TPU v7x, 512 devices: a whole 4x4x16 slice. The times are simulated.
512 devices in a mesh: tm: 16 (over y, x), chan: 32 (over z, core).
Axes of the slice: x: 4, y: 4, z: 16, core: 2. Of those that a mesh axis runs over, the one named last changes fastest.
Arguments:
- records: bfloat16 [128, 1024, 4096], P('tm', None, 'chan'), may hold values from -6 to 6
- pair_list: int32 [2, 32768], P(None, 'chan'), may hold values from 0 to 4095, as said below
- live_count: int32 [32], P('chan'), may hold values from 256 to 1024
Outputs:
- stacks: float32 [2, 256, 32768], P(None, 'tm', 'chan')
Inputs may be any that keep to these rules, and one draw needn't show every extreme that they name: pair_list[0, p] lies in channel block p // 1024 (block b holds channels b * 128 to (b + 1) * 128 - 1); pair_list[1, p] lies in a block at most 1 block from it.
All inputs are finite; a program needn't handle non-finite values.
Results may differ from a plain program's by a relative error of at most 0.0047.
Values may be sent and summed in bfloat16 or wider, within the bound.
A program may use at most 64 MiB of HBM per device.

v0:
```python
import math

import jax
import jax.numpy as jnp
from jax import lax
from jax.sharding import PartitionSpec as P

SAMPLES = 1024
NF = 256
BAND_LO = 16
REACH = 1


EPSILON = 1e-06


def extended_2(block, sides, width):
    for axis, dim in sides:
        count = lax.axis_size(axis)
        forward = [(i, i + 1) for i in range(count - 1)]
        backward = [(target, source) for source, target in forward]
        low = lax.ppermute(
            lax.slice_in_dim(block, block.shape[dim] - width, None, axis=dim), axis, forward
        )
        high = lax.ppermute(lax.slice_in_dim(block, 0, width, axis=dim), axis, backward)
        block = jnp.concatenate([low, block, high], axis=dim)
    return block


def fourier_table(samples, band_bins, lowest):
    sample_ids = jnp.arange(samples, dtype=jnp.int32)
    bin_ids = jnp.arange(band_bins, dtype=jnp.int32) + lowest
    phases = bin_ids[:, None] * sample_ids[None, :] % samples
    angles = phases.astype(jnp.float32) * (2.0 * math.pi / samples)
    tapers = 0.5 - 0.5 * jnp.cos(sample_ids.astype(jnp.float32) * (2.0 * math.pi / samples))
    real_part = jnp.cos(angles) * tapers[None, :]
    imag_part = -jnp.sin(angles) * tapers[None, :]
    return jnp.concatenate([real_part, imag_part], axis=0).astype(jnp.bfloat16)


def cross_sum(own_block, extended, left_select, right_select, group):
    count = extended.shape[0]
    own_blocks = own_block.reshape((count // group, group) + own_block.shape[1:])
    wide_blocks = extended.reshape((count // group, group) + extended.shape[1:])

    def accumulate(running, pieces):
        own_piece, wide_piece = pieces
        left_part = jnp.einsum(
            "gknc,cp->gknp", own_piece, left_select, preferred_element_type=jnp.float32
        )
        right_part = jnp.einsum(
            "gknc,cp->gknp", wide_piece, right_select, preferred_element_type=jnp.float32
        )
        real_part = jnp.sum(
            left_part[:, 0] * right_part[:, 0] + left_part[:, 1] * right_part[:, 1], axis=0
        )
        imag_part = jnp.sum(
            left_part[:, 1] * right_part[:, 0] - left_part[:, 0] * right_part[:, 1], axis=0
        )
        return (running + jnp.stack([real_part, imag_part]), None)

    initial = jnp.zeros((2, extended.shape[2], left_select.shape[1]), jnp.float32)
    totals, unused = lax.scan(accumulate, initial, (own_blocks, wide_blocks))
    return totals


def body(records, pair_list, live_count):
    seg_dev, samples, chan_dev = records.shape
    basis_table = fourier_table(SAMPLES, NF, BAND_LO)
    spectrum = jnp.einsum("fl,slc->sfc", basis_table, records, preferred_element_type=jnp.float32)
    powers = jnp.sum(spectrum * spectrum, axis=1, keepdims=True) / NF
    whitened = (spectrum * lax.rsqrt(powers + EPSILON)).astype(jnp.bfloat16)
    whitened = whitened.reshape(seg_dev, 2, NF, chan_dev)
    extended = extended_2(whitened, (("chan", 3),), REACH * chan_dev)
    block_index = lax.axis_index("chan")
    own_anchor = block_index * chan_dev
    wide_anchor = (block_index - REACH) * chan_dev
    left_local = pair_list[0] - own_anchor
    right_local = pair_list[1] - wide_anchor
    own_ids = jnp.arange(chan_dev, dtype=jnp.int32)
    wide_ids = jnp.arange(extended.shape[3], dtype=jnp.int32)
    left_select = (own_ids[:, None] == left_local[None, :]).astype(jnp.bfloat16)
    right_select = (wide_ids[:, None] == right_local[None, :]).astype(jnp.bfloat16)
    group = math.gcd(extended.shape[0], max(1, NF // extended.shape[2]))
    totals = cross_sum(whitened, extended, left_select, right_select, group)
    totals = lax.psum_scatter(totals, "tm", scatter_dimension=1, tiled=True)
    slot_mask = (jnp.arange(pair_list.shape[1], dtype=jnp.int32) < live_count[0]).astype(
        jnp.float32
    )
    segment_total = seg_dev * lax.axis_size("tm")
    return totals / segment_total * slot_mask[None, None, :]


def solution(mesh):
    in_specs = (P("tm", None, "chan"), P(None, "chan"), P("chan"))
    out_specs = P(None, "tm", "chan")
    return jax.shard_map(body, mesh=mesh, in_specs=in_specs, out_specs=out_specs, check_vma=False)
```

profile of v0, /device:TPU:1, one launch (start us, length us, event | category | flops | bytes accessed | tf_op | source)
XLA Modules:
  0.0 204.5 jit_solution(2405901401265729940)
XLA Ops:
  6.5 0.0 copy-start
  6.5 0.0 reduce-scatter.2.cloned.1.call-start
  6.6 4.6 %multiply_convert_fusion.2 = (bf16[256,1024]{1,0:T(8,128)(2,1)S(1)}, bf16[256,1024]{1,0:T(8,128)(2,1)S(1)}) fusion(f32[1024]{0:T(1024)S(1)} %multiply_subtract_fusion, s32[256]{0:T(256)S(1)} %iota_add_fusion), kind=kLoop, calls=%fused_computation.35 | loop fusion | flops 4980736 | bytes 1053696 | tf_op jit(solution)/shard_map/convert
  11.2 0.0 copy-done
  11.2 1.3 multiply_reduce_fusion
  12.5 0.0 copy-start.1
  12.5 1.2 multiply_convert_fusion
  13.7 4.9 %collective-permute-start = (bf16[8,2,256,128]{3,2,1,0:T(8,128)(2,1)}, bf16[8,2,256,128]{3,2,1,0:T(8,128)(2,1)S(1)}, u32[]{:S(2)}, u32[]{:S(2)}) collective-permute-start(bf16[8,2,256,128]{3,2,1,0:T(8,128)(2,1)} %bitcast.4), channel_id=1, source_target_pairs={{0,1},{1,2},{2,3},{3,4},{4,5},{5,6},{6,7},{7,8},{8,9},{9,10},{10,1... | collective-permute-start | bytes 3145736 | tf_op jit(solution)/shard_map/ppermute | solution.py:22
  18.6 5.2 %collective-permute-start.1 = (bf16[8,2,256,128]{3,2,1,0:T(8,128)(2,1)}, bf16[8,2,256,128]{3,2,1,0:T(8,128)(2,1)}, u32[]{:S(2)}, u32[]{:S(2)}) collective-permute-start(bf16[8,2,256,128]{3,2,1,0:T(8,128)(2,1)} %bitcast.4), channel_id=1, source_target_pairs={{1,0},{2,1},{3,2},{4,3},{5,4},{6,5},{7,6},{8,7},{9,8},{10,9},{11,1... | collective-permute-start | bytes 3145736 | tf_op jit(solution)/shard_map/ppermute | solution.py:25
  23.9 0.0 copy-done.1
  23.9 6.8 %collective-permute-done = bf16[8,2,256,128]{3,2,1,0:T(8,128)(2,1)S(1)} collective-permute-done((bf16[8,2,256,128]{3,2,1,0:T(8,128)(2,1)}, bf16[8,2,256,128]{3,2,1,0:T(8,128)(2,1)S(1)}, u32[]{:S(2)}, u32[]{:S(2)}) %collective-permute-start) | collective-permute-done | bytes 1048608 | tf_op jit(solution)/shard_map/ppermute | solution.py:22
  30.7 4.4 %collective-permute-done.1 = bf16[8,2,256,128]{3,2,1,0:T(8,128)(2,1)} collective-permute-done((bf16[8,2,256,128]{3,2,1,0:T(8,128)(2,1)}, bf16[8,2,256,128]{3,2,1,0:T(8,128)(2,1)}, u32[]{:S(2)}, u32[]{:S(2)}) %collective-permute-start.1) | collective-permute-done | bytes 1048608 | tf_op jit(solution)/shard_map/ppermute | solution.py:25
  35.1 3.7 %maximum_bitcast_fusion = bf16[8,1,2,256,384]{4,3,2,1,0:T(8,128)(2,1)} fusion(bf16[8,2,256,128]{3,2,1,0:T(8,128)(2,1)} %collective-permute-done.1, bf16[8,2,256,128]{3,2,1,0:T(8,128)(2,1)} %bitcast.4, bf16[8,2,256,128]{3,2,1,0:T(8,128)(2,1)S(1)} %collective-permute-done), kind=kLoop, calls=%fused_computation.21 | loop fusion | flops 9437184 | bytes 6291456 | tf_op jit(solution)/shard_map/reshape | solution.py:44
  38.8 65.3 %while.11 = (s32[]{:T(128)}, f32[2,256,1024]{2,1,0:T(8,128)}, bf16[8,1,2,256,128]{4,3,2,1,0:T(8,128)(2,1)}, bf16[8,1,2,256,384]{4,3,2,1,0:T(8,128)(2,1)}, s32[10...) while((s32[]{:T(128)}, f32[2,256,1024]{2,1,0:T(8,128)}, ...), condition=%wide.region_2.3_spmd.clone, body=%wide.region_1.2_spmd.clone.sunk | while | flops 541065216 | bytes 17310816 | solution.py:63
  38.8 1.7 convolution_bitcast_fusion.4
  40.5 1.3 convolution_bitcast_fusion.5
  41.8 1.4 add_bitcast_fusion.2
  43.2 3.1 %maximum_add_fusion.2 = f32[2,256,1024]{2,1,0:T(8,128)} fusion(f32[1,256,1024]{2,1,0:T(8,128)} %get-tuple-element.130, f32[1,256,1024]{2,1,0:T(8,128)S(1)} %get-tuple-element.131, f32[2,256,1024]{2,1,0:T(8,128)} %get-tuple-element.141, pred[]{:T(512)S(6)} %compare.4), kind=kLoop, calls=%fused_computation.2.clone.1 | loop fusion | flops 1572864 | bytes 6291457 | tf_op jit(solution)/shard_map/while/body/eval_jaxpr/add | solution.py:60
  46.3 1.7 convolution_bitcast_fusion.4
  48.0 1.3 convolution_bitcast_fusion.5
  49.4 1.4 add_bitcast_fusion.2
  50.8 3.8 %maximum_add_fusion.2 = f32[2,256,1024]{2,1,0:T(8,128)} fusion(f32[1,256,1024]{2,1,0:T(8,128)} %get-tuple-element.130, f32[1,256,1024]{2,1,0:T(8,128)S(1)} %get-tuple-element.131, f32[2,256,1024]{2,1,0:T(8,128)} %get-tuple-element.141, pred[]{:T(512)S(6)} %compare.4), kind=kLoop, calls=%fused_computation.2.clone.1 | loop fusion | flops 1572864 | bytes 6291457 | tf_op jit(solution)/shard_map/while/body/eval_jaxpr/add | solution.py:60
  54.6 1.7 convolution_bitcast_fusion.4
  56.3 1.3 convolution_bitcast_fusion.5
  57.6 1.4 add_bitcast_fusion.2
  59.0 3.8 %maximum_add_fusion.2 = f32[2,256,1024]{2,1,0:T(8,128)} fusion(f32[1,256,1024]{2,1,0:T(8,128)} %get-tuple-element.130, f32[1,256,1024]{2,1,0:T(8,128)S(1)} %get-tuple-element.131, f32[2,256,1024]{2,1,0:T(8,128)} %get-tuple-element.141, pred[]{:T(512)S(6)} %compare.4), kind=kLoop, calls=%fused_computation.2.clone.1 | loop fusion | flops 1572864 | bytes 6291457 | tf_op jit(solution)/shard_map/while/body/eval_jaxpr/add | solution.py:60
  62.8 1.7 convolution_bitcast_fusion.4
  64.5 1.3 convolution_bitcast_fusion.5
  65.9 1.4 add_bitcast_fusion.2
  67.3 3.8 %maximum_add_fusion.2 = f32[2,256,1024]{2,1,0:T(8,128)} fusion(f32[1,256,1024]{2,1,0:T(8,128)} %get-tuple-element.130, f32[1,256,1024]{2,1,0:T(8,128)S(1)} %get-tuple-element.131, f32[2,256,1024]{2,1,0:T(8,128)} %get-tuple-element.141, pred[]{:T(512)S(6)} %compare.4), kind=kLoop, calls=%fused_computation.2.clone.1 | loop fusion | flops 1572864 | bytes 6291457 | tf_op jit(solution)/shard_map/while/body/eval_jaxpr/add | solution.py:60
  71.1 1.7 convolution_bitcast_fusion.4
  72.8 1.3 convolution_bitcast_fusion.5
  74.1 1.4 add_bitcast_fusion.2
  75.5 3.8 %maximum_add_fusion.2 = f32[2,256,1024]{2,1,0:T(8,128)} fusion(f32[1,256,1024]{2,1,0:T(8,128)} %get-tuple-element.130, f32[1,256,1024]{2,1,0:T(8,128)S(1)} %get-tuple-element.131, f32[2,256,1024]{2,1,0:T(8,128)} %get-tuple-element.141, pred[]{:T(512)S(6)} %compare.4), kind=kLoop, calls=%fused_computation.2.clone.1 | loop fusion | flops 1572864 | bytes 6291457 | tf_op jit(solution)/shard_map/while/body/eval_jaxpr/add | solution.py:60
  79.3 1.7 convolution_bitcast_fusion.4
  81.0 1.3 convolution_bitcast_fusion.5
  82.4 1.4 add_bitcast_fusion.2
  83.8 3.8 %maximum_add_fusion.2 = f32[2,256,1024]{2,1,0:T(8,128)} fusion(f32[1,256,1024]{2,1,0:T(8,128)} %get-tuple-element.130, f32[1,256,1024]{2,1,0:T(8,128)S(1)} %get-tuple-element.131, f32[2,256,1024]{2,1,0:T(8,128)} %get-tuple-element.141, pred[]{:T(512)S(6)} %compare.4), kind=kLoop, calls=%fused_computation.2.clone.1 | loop fusion | flops 1572864 | bytes 6291457 | tf_op jit(solution)/shard_map/while/body/eval_jaxpr/add | solution.py:60
  87.6 1.7 convolution_bitcast_fusion.4
  89.3 1.3 convolution_bitcast_fusion.5
  90.6 1.4 add_bitcast_fusion.2
  92.0 3.8 %maximum_add_fusion.2 = f32[2,256,1024]{2,1,0:T(8,128)} fusion(f32[1,256,1024]{2,1,0:T(8,128)} %get-tuple-element.130, f32[1,256,1024]{2,1,0:T(8,128)S(1)} %get-tuple-element.131, f32[2,256,1024]{2,1,0:T(8,128)} %get-tuple-element.141, pred[]{:T(512)S(6)} %compare.4), kind=kLoop, calls=%fused_computation.2.clone.1 | loop fusion | flops 1572864 | bytes 6291457 | tf_op jit(solution)/shard_map/while/body/eval_jaxpr/add | solution.py:60
  95.8 1.7 convolution_bitcast_fusion.4
  97.5 1.3 convolution_bitcast_fusion.5
  98.9 1.4 add_bitcast_fusion.2
  100.3 3.8 %maximum_add_fusion.2 = f32[2,256,1024]{2,1,0:T(8,128)} fusion(f32[1,256,1024]{2,1,0:T(8,128)} %get-tuple-element.130, f32[1,256,1024]{2,1,0:T(8,128)S(1)} %get-tuple-element.131, f32[2,256,1024]{2,1,0:T(8,128)} %get-tuple-element.141, pred[]{:T(512)S(6)} %compare.4), kind=kLoop, calls=%fused_computation.2.clone.1 | loop fusion | flops 1572864 | bytes 6291457 | tf_op jit(solution)/shard_map/while/body/eval_jaxpr/add | solution.py:60
  104.1 0.0 reduce-scatter.2.cloned.1.call-update
  104.8 91.3 %reduce-scatter.2.cloned.1.call-done = f32[2,16,1024]{2,1,0:T(8,128)} async-done(((f32[2,256,1024]{2,1,0:T(8,128)}), f32[2,16,1024]{2,1,0:T(8,128)}) %reduce-scatter.2.cloned.1.call-update) | async-done | bytes 131088 | tf_op jit(solution)/shard_map/reduce_scatter | solution.py:86
  196.1 1.6 broadcast_multiply_fusion
  (6 shorter events, 0.1 us)
Async XLA Ops:
  6.5 4.7 %copy-start = (bf16[8,1024,128]{2,1,0:T(8,128)(2,1)S(1)}, bf16[8,1024,128]{2,1,0:T(8,128)(2,1)}, u32[]{:S(2)}) copy-start(bf16[8,1024,128]{2,1,0:T(8,128)(2,1)} %param.5) | copy-start | bytes 6291460
  6.5 189.6 %reduce-scatter.2.cloned.1.call-start = ((), (), s32[]{:S(2)}) async-start(), calls=%async_computation.1 | async-start | bytes 2228224 | tf_op jit(solution)/shard_map/reduce_scatter | solution.py:86
  12.5 11.4 %copy-start.1 = (s32[2,1024]{1,0:T(2,128)S(1)}, s32[2,1024]{1,0:T(2,128)}, u32[]{:S(2)}) copy-start(s32[2,1024]{1,0:T(2,128)} %param.6) | copy-start | bytes 24580
  13.7 17.0 %collective-permute-start = (bf16[8,2,256,128]{3,2,1,0:T(8,128)(2,1)}, bf16[8,2,256,128]{3,2,1,0:T(8,128)(2,1)S(1)}, u32[]{:S(2)}, u32[]{:S(2)}) collective-permute-start(bf16[8,2,256,128]{3,2,1,0:T(8,128)(2,1)} %bitcast.4), channel_id=1, source_target_pairs={{0,1},{1,2},{2,3},{3,4},{4,5},{5,6},{6,7},{7,8},{8,9},{9,10},{10,1... | collective-permute-start | bytes 3145736 | tf_op jit(solution)/shard_map/ppermute | solution.py:22
  18.6 16.4 %collective-permute-start.1 = (bf16[8,2,256,128]{3,2,1,0:T(8,128)(2,1)}, bf16[8,2,256,128]{3,2,1,0:T(8,128)(2,1)}, u32[]{:S(2)}, u32[]{:S(2)}) collective-permute-start(bf16[8,2,256,128]{3,2,1,0:T(8,128)(2,1)} %bitcast.4), channel_id=1, source_target_pairs={{1,0},{2,1},{3,2},{4,3},{5,4},{6,5},{7,6},{8,7},{9,8},{10,9},{11,1... | collective-permute-start | bytes 3145736 | tf_op jit(solution)/shard_map/ppermute | solution.py:25
Sparse Core Ops, SparseCore 0:
  104.2 91.8 reduce-scatter.1
where the time goes:
time: 206 us; the launch traced here: 205 us
  waiting for transfers between devices  103 us (50%)
  other arithmetic  52 us (25%)
  matrix products  25.6 us (12%)
  between operations  14.1 us (7%)
  starting transfers between devices  10.1 us (5%)
    reduce_scatter x1, waiting for transfers between devices, body(): totals = lax.psum_scatter(totals, 'tm', scatter_dimension=1, tiled=True)  91.3 us
    add x8, other arithmetic, accumulate(): return (running + jnp.stack([real_part, imag_part]), None)  29.5 us
    dot_general x8, matrix products, accumulate(): jnp.einsum('gknc,cp->gknp', wide_piece, right_select, preferred_element_t...  13.7 us
    add x8, other arithmetic, accumulate(): left_part[:, 0] * right_part[:, 0] + left_part[:, 1] * right_part[:, 1]  11.4 us
    dot_general x8, matrix products, accumulate(): jnp.einsum('gknc,cp->gknp', own_piece, left_select, preferred_element_typ...  10.7 us
    ppermute x1, waiting for transfers between devices, extended_2(): lax.ppermute(lax.slice_in_dim(block, block.shape[dim] - width, None, axis...  6.77 us
    ppermute x1, starting transfers between devices, extended_2(): lax.ppermute(lax.slice_in_dim(block, 0, width, axis=dim), axis, backward)  5.21 us
    ppermute x1, starting transfers between devices, extended_2(): lax.ppermute(lax.slice_in_dim(block, block.shape[dim] - width, None, axis...  4.92 us
  transfers between devices with their start and end apart: 3, of which 3 were waited for; matrix products, arithmetic and copies ran while one was open for 0% of the time, Pallas kernels for 0%

commit v1 on v0

v1 whole, which is shorter than its diff:
```python
import math

import jax
import jax.numpy as jnp
import ml_dtypes
import numpy as np
from jax import lax
from jax.experimental import pallas as pl
from jax.experimental.pallas import tpu as pltpu
from jax.sharding import PartitionSpec as P

SAMPLES = 1024
NF = 256
BAND_LO = 16
EPSILON = 1e-06

SIDE = 4
SEG = 8
CH = 128
PAIRS = 1024
CHUNKS = 8
ROWS = 2 * NF // CHUNKS
TILE = 256
TILES = PAIRS // TILE
MESH = pl.DeviceIdType.MESH


def basis_rows():
    sample_ids = np.arange(SAMPLES, dtype=np.int64)
    bin_ids = np.arange(NF, dtype=np.int64) + BAND_LO
    phases = bin_ids[:, None] * sample_ids[None, :] % SAMPLES
    step = np.float32(2.0 * math.pi / SAMPLES)
    angles = phases.astype(np.float32) * step
    tapers = np.float32(0.5) - np.float32(0.5) * np.cos(sample_ids.astype(np.float32) * step)
    table = np.stack([np.cos(angles) * tapers[None, :], -np.sin(angles) * tapers[None, :]])
    table = table.reshape(2, SIDE, SIDE, CHUNKS, 2, SAMPLES)
    parts = []
    for k in range(CHUNKS):
        part = table[:, :, :, k]
        if k % 2 == 0:
            part = part.transpose(0, 2, 1, 3, 4)
        parts.append(part.reshape(ROWS, SAMPLES))
    return np.concatenate(parts, axis=0).astype(np.float32).astype(ml_dtypes.bfloat16)


def kernel(
    basis_hbm, rec_hbm, pair_hbm, live_hbm, out_ref,
    basis, rec, pair, live, own, low, high, w_left, w_right,
    part, send1, recv1, part2, send2, recv2,
    in_sem, z_send, z_recv, p1_send, p1_recv, p2_send, p2_recv,
):
    t = lax.axis_index("tm")
    c = lax.axis_index("chan")
    n_chan = lax.axis_size("chan")
    y, x = lax.div(t, SIDE), lax.rem(t, SIDE)
    c_high = lax.rem(c + 1, n_chan)
    c_low = lax.rem(c + n_chan - 1, n_chan)

    pair_copy = pltpu.make_async_copy(pair_hbm, pair, in_sem.at[0])
    live_copy = pltpu.make_async_copy(live_hbm, live, in_sem.at[1])
    basis_copy = pltpu.make_async_copy(basis_hbm, basis, in_sem.at[2])
    rec_copies = [
        pltpu.make_async_copy(rec_hbm.at[pl.ds(2 * q, 2)], rec.at[pl.ds(2 * q, 2)], in_sem.at[3 + q])
        for q in range(SEG // 2)
    ]
    rec_copies[0].start()
    basis_copy.start()
    for q in range(1, SEG // 2):
        rec_copies[q].start()
    pair_copy.start()
    live_copy.start()

    def x_peer(d):
        return y * SIDE + lax.rem(x + d, SIDE)

    def y_peer(d):
        return lax.rem(y + d, SIDE) * SIDE + x

    barrier = pltpu.get_barrier_semaphore()
    for peer in (c_low, c_high):
        pl.semaphore_signal(barrier, inc=1, device_id=(t, peer), device_id_type=MESH)
    for d in range(1, SIDE):
        pl.semaphore_signal(barrier, inc=1, device_id=(x_peer(d), c), device_id_type=MESH)
        pl.semaphore_signal(barrier, inc=1, device_id=(y_peer(d), c), device_id_type=MESH)

    def z_copies(k, q):
        if q is None:
            piece, sem = (k,), k + 3
        else:
            piece, sem = (k, pl.ds(2 * q, 2)), q
        return [
            pltpu.make_async_remote_copy(
                src_ref=own.at[piece],
                dst_ref=landing.at[piece],
                send_sem=z_send.at[way, sem],
                recv_sem=z_recv.at[way, sem],
                device_id=(t, peer),
                device_id_type=MESH,
            )
            for way, landing, peer in ((0, high, c_low), (1, low, c_high))
        ]

    z_started = {}
    basis_copy.wait()
    for q in range(SEG // 2):
        rec_copies[q].wait()
        wide = jnp.concatenate([rec[2 * q], rec[2 * q + 1]], axis=1)
        spectrum = jnp.dot(basis[...], wide, preferred_element_type=jnp.float32)
        powers = jnp.sum(spectrum * spectrum, axis=0, keepdims=True) / NF
        white = (spectrum * lax.rsqrt(powers + EPSILON)).astype(jnp.bfloat16)
        white = white.reshape(CHUNKS, ROWS, 2 * CH)
        own[:, 2 * q] = white[:, :, :CH]
        own[:, 2 * q + 1] = white[:, :, CH:]
        if q == 0:
            pl.semaphore_wait(barrier, 2 + 2 * (SIDE - 1))
        z_started[0, q] = z_copies(0, q)
        for copy in z_started[0, q]:
            copy.start()
    for k in range(1, CHUNKS):
        z_started[k, None] = z_copies(k, None)
        for copy in z_started[k, None]:
            copy.start()

    pair_copy.wait()
    live_copy.wait()
    n_live = live[0]
    for n in range(TILES):
        cols = pl.ds(n * TILE, TILE)
        left = pair[0:1, cols] - c * CH
        right = pair[1:2, cols] - (c - 1) * CH
        slots = lax.broadcasted_iota(jnp.int32, (1, TILE), 1) + n * TILE
        left = jnp.where(slots < n_live, left, -1)
        ids = lax.broadcasted_iota(jnp.int32, (CH, TILE), 0)
        w_left[n] = jnp.where(ids == left, 1.0 / 128.0, 0.0).astype(jnp.bfloat16)
        for place, block in ((0, 1), (1, 0), (2, 2)):
            hot = jnp.where(ids + block * CH == right, 1.0, 0.0)
            w_right[n, pl.ds(place * CH, CH)] = hot.astype(jnp.bfloat16)

    half = ROWS // 2
    group = half // SIDE

    def multiply(k):
        def step(n, carry):
            mine = own[k].reshape(SEG * ROWS, CH)
            wide = jnp.concatenate(
                [mine, low[k].reshape(SEG * ROWS, CH), high[k].reshape(SEG * ROWS, CH)], axis=1
            )
            left = jnp.dot(mine, w_left[n], preferred_element_type=jnp.float32)
            right = jnp.dot(wide, w_right[n], preferred_element_type=jnp.float32)
            left = left.reshape(SEG, 2, half, TILE)
            right = right.reshape(SEG, 2, half, TILE)
            real = jnp.sum(left[:, 0] * right[:, 0] + left[:, 1] * right[:, 1], axis=0)
            imag = jnp.sum(left[:, 1] * right[:, 0] - left[:, 0] * right[:, 1], axis=0)
            cols = pl.ds(pl.multiple_of(n * TILE, TILE), TILE)
            for a in range(SIDE):
                rows = slice(a * group, (a + 1) * group)
                both = jnp.concatenate([real[rows], imag[rows]], axis=0)
                part[k % 2, a, :, cols] = both
                send1[k, a, :, cols] = both.astype(jnp.bfloat16)
            return carry

        lax.fori_loop(0, TILES, step, 0)

    def first(k):
        return (x, x_peer) if k % 2 == 0 else (y, y_peer)

    def second(k):
        return (y, y_peer) if k % 2 == 0 else (x, x_peer)

    def exchange(k, phase):
        place, peer = first(k) if phase == 1 else second(k)
        source, landing = (send1, recv1) if phase == 1 else (send2, recv2)
        sends, recvs = (p1_send, p1_recv) if phase == 1 else (p2_send, p2_recv)
        copies = [
            pltpu.make_async_remote_copy(
                src_ref=source.at[k, lax.rem(place + d, SIDE)],
                dst_ref=landing.at[k, d - 1],
                send_sem=sends.at[k, d - 1],
                recv_sem=recvs.at[k, d - 1],
                device_id=(peer(d), c),
                device_id_type=MESH,
            )
            for d in (2, 1, 3)
        ]
        for copy in copies:
            copy.start()
        return copies

    def add_first(k):
        place, _ = first(k)
        total = part[k % 2, place]
        for d in range(SIDE - 1):
            total = total + recv1[k, d].astype(jnp.float32)
        for b in range(SIDE):
            pieces = []
            for g in range(TILES):
                cols = slice(g * TILE, (g + 1) * TILE)
                pieces.append(total[2 * b:2 * b + 2, cols])
                pieces.append(total[group + 2 * b:group + 2 * b + 2, cols])
            both = jnp.concatenate(pieces, axis=0)
            part2[k % 2, b] = both
            send2[k, b] = both.astype(jnp.bfloat16)

    def add_second(k):
        place, _ = second(k)
        total = part2[k % 2, place]
        for d in range(SIDE - 1):
            total = total + recv2[k, d].astype(jnp.float32)
        for g in range(TILES):
            cols = pl.ds(g * TILE, TILE)
            out_ref[0, 2 * k:2 * k + 2, cols] = total[4 * g:4 * g + 2]
            out_ref[1, 2 * k:2 * k + 2, cols] = total[4 * g + 2:4 * g + 4]

    phase1, phase2 = {}, {}

    def finish_first(k):
        for copy in phase1[k]:
            copy.wait()
        add_first(k)
        phase2[k] = exchange(k, 2)

    def finish_second(k):
        for copy in phase2[k]:
            copy.wait()
        add_second(k)

    for k in range(CHUNKS):
        for copies in [z_started[key] for key in z_started if key[0] == k]:
            for copy in copies:
                copy.wait()
        multiply(k)
        phase1[k] = exchange(k, 1)
        if k >= 1:
            finish_first(k - 1)
        if k >= 2:
            finish_second(k - 2)
    finish_first(CHUNKS - 1)
    finish_second(CHUNKS - 2)
    finish_second(CHUNKS - 1)


def body(records, pair_list, live_count):
    table = jnp.asarray(basis_rows())
    any_space = pl.BlockSpec(memory_space=pl.ANY)
    vmem, bf16, f32 = pltpu.VMEM, jnp.bfloat16, jnp.float32
    dma = pltpu.SemaphoreType.DMA
    group = ROWS // SIDE
    return pl.pallas_call(
        kernel,
        out_shape=jax.ShapeDtypeStruct((2, 2 * CHUNKS, PAIRS), f32),
        in_specs=[any_space] * 4,
        out_specs=pl.BlockSpec(memory_space=vmem),
        scratch_shapes=[
            vmem((2 * NF, SAMPLES), bf16),
            vmem((SEG, SAMPLES, CH), bf16),
            vmem((2, PAIRS), jnp.int32),
            pltpu.SMEM((1,), jnp.int32),
            vmem((CHUNKS, SEG, ROWS, CH), bf16),
            vmem((CHUNKS, SEG, ROWS, CH), bf16),
            vmem((CHUNKS, SEG, ROWS, CH), bf16),
            vmem((TILES, CH, TILE), bf16),
            vmem((TILES, 3 * CH, TILE), bf16),
            vmem((2, SIDE, group, PAIRS), f32),
            vmem((CHUNKS, SIDE, group, PAIRS), bf16),
            vmem((CHUNKS, SIDE - 1, group, PAIRS), bf16),
            vmem((2, SIDE, group, TILE), f32),
            vmem((CHUNKS, SIDE, group, TILE), bf16),
            vmem((CHUNKS, SIDE - 1, group, TILE), bf16),
            dma((3 + SEG // 2,)),
            dma((2, CHUNKS + 3)),
            dma((2, CHUNKS + 3)),
            dma((CHUNKS, SIDE - 1)),
            dma((CHUNKS, SIDE - 1)),
            dma((CHUNKS, SIDE - 1)),
            dma((CHUNKS, SIDE - 1)),
        ],
        compiler_params=pltpu.CompilerParams(
            collective_id=0, has_side_effects=True, vmem_limit_bytes=56 * 2**20
        ),
        cost_estimate=pl.CostEstimate(
            flops=7 * 10**9, bytes_accessed=4 * 2**20, transcendentals=0
        ),
    )(table, records, pair_list, live_count)


def solution(mesh):
    in_specs = (P("tm", None, "chan"), P(None, "chan"), P("chan"))
    out_specs = P(None, "tm", "chan")
    return jax.shard_map(body, mesh=mesh, in_specs=in_specs, out_specs=out_specs, check_vma=False)
```

time: 206 us -> 51.4 us (0.25)
  the two profiles are of different devices: /device:TPU:1 before, /device:TPU:2 now
where the time goes in v1:
time: 51.4 us; the launch traced here: 51.3 us
  Pallas kernels  49 us (95%)
  local copies, waits for them, and re-layouts  1.57 us (3%)
  between operations  0.66 us (1%)
    pallas_call x1, Pallas kernels, body(): pl.pallas_call(kernel, out_shape=jax.ShapeDtypeStruct((2, 2 * CHUNKS, PAI...  49 us
    unnamed x1, local copies, waits for them, and re-layouts  1.57 us

profile of v1, /device:TPU:2, one launch (start us, length us, event | category | flops | bytes accessed | tf_op | source)
XLA Modules:
  0.0 51.3 jit_solution(1489784612503398167)
XLA Ops:
  0.7 49.0 %shard_map.46 = f32[2,16,1024]{2,1,0:T(8,128)} custom-call(bf16[512,1024]{1,0:T(8,128)(2,1)} %constant.2.clone.basis_hbm, bf16[8,1024,128]{2,1,0:T(8,128)(2,1)} %rec_hbm.1, s32[2,1024]{1,0:T(2,128)} %pair_hbm.1, s32[1]{0:T(128)S(6)} %copy.6.live_hbm), custom_call_target="tpu_custom_call" | custom-call | flops 7000000000 | bytes 4194304 | tf_op jit(solution)/shard_map/pallas_call | solution.py:248
  49.7 1.6 %copy.7 = f32[2,16,1024]{2,1,0:T(8,128)} copy(f32[2,16,1024]{2,1,0:T(8,128)} %shard_map.46) | data formatting | bytes 262144

commit v2 on v0

v2 whole, which is shorter than its diff:
```python
import math

import jax
import jax.numpy as jnp
import ml_dtypes
import numpy as np
from jax import lax
from jax.experimental import pallas as pl
from jax.experimental.pallas import tpu as pltpu
from jax.sharding import PartitionSpec as P

SAMPLES = 1024
NF = 256
BAND_LO = 16
EPSILON = 1e-06

SIDE = 4
OWNERS = SIDE * SIDE
SEG = 8
CH = 128
PAIRS = 1024
BINS = 8
ROWS = 2 * BINS
TILE = 256
TILES = PAIRS // TILE
QUADS = SEG // 2
MESH = pl.DeviceIdType.MESH


def basis_tables():
    sample_ids = np.arange(SAMPLES, dtype=np.int64)
    bin_ids = np.arange(NF, dtype=np.int64) + BAND_LO
    phases = bin_ids[:, None] * sample_ids[None, :] % SAMPLES
    step = np.float32(2.0 * math.pi / SAMPLES)
    angles = phases.astype(np.float32) * step
    tapers = np.float32(0.5) - np.float32(0.5) * np.cos(sample_ids.astype(np.float32) * step)
    table = np.stack([np.cos(angles) * tapers[None, :], -np.sin(angles) * tapers[None, :]])
    table = table.astype(np.float32).astype(ml_dtypes.bfloat16)
    table = table.reshape(2, SIDE, SIDE, 2, BINS, SAMPLES).transpose(3, 1, 2, 0, 4, 5)
    table = table.reshape(2, SIDE, SIDE, ROWS, SAMPLES)
    ids = np.arange(2 * SIDE - 1) % SIDE
    first = table[0][ids[None, :], (ids[:, None] + ids[None, :]) % SIDE]
    second = table[1][ids[:, None], ids[None, :]]
    return first, second


def kernel(
    basis_a_hbm, basis_b_hbm, rec_hbm, pair_hbm, live_hbm, out_ref,
    basis, rec, pair, live, w_left, w_right,
    own_a, low_a, high_a, stage_b, own_b, low_b, high_b, own_sum, send_sum, recv_sum, total_b,
    in_sem, za_send, za_recv, zb_send, zb_recv, gather_send, gather_recv, sum_send, sum_recv,
):
    t = lax.axis_index("tm")
    c = lax.axis_index("chan")
    n_chan = lax.axis_size("chan")
    y, x = lax.div(t, SIDE), lax.rem(t, SIDE)
    c_high = lax.rem(c + 1, n_chan)
    c_low = lax.rem(c + n_chan - 1, n_chan)
    ways = ((0, high_a, high_b, c_low), (1, low_a, low_b, c_high))

    def peer(dy, dx):
        return (lax.rem(y + dy, SIDE) * SIDE + lax.rem(x + dx, SIDE), c)

    others = [(dy, dx) for dy in (2, 1, 3, 0) for dx in (2, 1, 3, 0) if (dy, dx) != (0, 0)]

    skew = lax.rem(x - y + SIDE, SIDE)
    basis_copies = [
        pltpu.make_async_copy(table.at[pl.ds(u, SIDE), pl.ds(v, SIDE)], basis.at[h], in_sem.at[2 + h])
        for h, (table, u, v) in enumerate(((basis_a_hbm, skew, y), (basis_b_hbm, y, x)))
    ]
    rec_copies = [
        pltpu.make_async_copy(rec_hbm.at[pl.ds(2 * q, 2)], rec.at[pl.ds(2 * q, 2)], in_sem.at[4 + q])
        for q in range(QUADS)
    ]
    pair_copy = pltpu.make_async_copy(pair_hbm, pair, in_sem.at[0])
    live_copy = pltpu.make_async_copy(live_hbm, live, in_sem.at[1])
    rec_copies[0].start()
    for copy in basis_copies:
        copy.start()
    for q in range(1, QUADS):
        rec_copies[q].start()
    pair_copy.start()
    live_copy.start()

    barrier = pltpu.get_barrier_semaphore()
    for to in [(t, c_low), (t, c_high)] + [peer(dy, dx) for dy, dx in others]:
        pl.semaphore_signal(barrier, inc=1, device_id=to, device_id_type=MESH)

    def send(source, landing, send_sem, recv_sem, to):
        copy = pltpu.make_async_remote_copy(
            src_ref=source,
            dst_ref=landing,
            send_sem=send_sem,
            recv_sem=recv_sem,
            device_id=to,
            device_id_type=MESH,
        )
        copy.start()
        return copy

    za, zb = {}, {}
    for copy in basis_copies:
        copy.wait()
    for q in range(QUADS):
        rec_copies[q].wait()
        wide = jnp.concatenate([rec[2 * q], rec[2 * q + 1]], axis=1)
        spectrum = jnp.dot(
            basis[...].reshape(2 * NF, SAMPLES), wide, preferred_element_type=jnp.float32
        )
        powers = jnp.sum(spectrum * spectrum, axis=0, keepdims=True) / NF
        white = (spectrum * lax.rsqrt(powers + EPSILON)).astype(jnp.bfloat16)
        for e in range(2):
            mine = white[:, e * CH:(e + 1) * CH].reshape(2, OWNERS, ROWS, CH)
            own_a[:, :, 2 * q + e] = mine[0].reshape(SIDE, SIDE, ROWS, CH)
            stage_b[q, :, e] = mine[1]
            own_b[q, 0, e] = mine[1, 0]
        if q == 0:
            pl.semaphore_wait(barrier, 2 + len(others))
        piece = (0, pl.ds(0, SIDE), pl.ds(2 * q, 2))
        for way, landing, _, to in ways:
            za[0, q, way] = send(
                own_a.at[piece], landing.at[piece], za_send.at[way, q], za_recv.at[way, q], (t, to)
            )
        for dy, dx in others:
            d = dy * SIDE + dx
            send(
                stage_b.at[q, d], own_b.at[q, d], gather_send.at[q], gather_recv.at[q], peer(dy, dx)
            )
    for k in range(1, SIDE):
        for way, landing, _, to in ways:
            sem = QUADS + k - 1
            za[k, 0, way] = send(
                own_a.at[k], landing.at[k], za_send.at[way, sem], za_recv.at[way, sem], (t, to)
            )

    pair_copy.wait()
    live_copy.wait()
    n_live = live[0]
    for n in range(TILES):
        cols = pl.ds(n * TILE, TILE)
        left = pair[0:1, cols] - c * CH
        right = pair[1:2, cols] - (c - 1) * CH
        slots = lax.broadcasted_iota(jnp.int32, (1, TILE), 1) + n * TILE
        left = jnp.where(slots < n_live, left, -1)
        ids = lax.broadcasted_iota(jnp.int32, (CH, TILE), 0)
        w_left[n] = jnp.where(ids == left, 1.0 / 128.0, 0.0).astype(jnp.bfloat16)
        for place, block in ((0, 1), (1, 0), (2, 2)):
            hot = jnp.where(ids + block * CH == right, 1.0, 0.0)
            w_right[n, pl.ds(place * CH, CH)] = hot.astype(jnp.bfloat16)

    def multiply(own, low, high, groups):
        mine = own.reshape(-1, CH)
        wide = jnp.concatenate([mine, low.reshape(-1, CH), high.reshape(-1, CH)], axis=1)
        shape = (groups, mine.shape[0] // (groups * ROWS), 2, BINS, TILE)
        sums = []
        for n in range(TILES):
            left = jnp.dot(mine, w_left[n], preferred_element_type=jnp.float32).reshape(shape)
            right = jnp.dot(wide, w_right[n], preferred_element_type=jnp.float32).reshape(shape)
            real = jnp.sum(left[:, :, 0] * right[:, :, 0] + left[:, :, 1] * right[:, :, 1], axis=1)
            imag = jnp.sum(left[:, :, 1] * right[:, :, 0] - left[:, :, 0] * right[:, :, 1], axis=1)
            sums.append(jnp.concatenate([real, imag], axis=1))
        return sums

    def tile(n):
        return pl.ds(n * TILE, TILE)

    def part_a(k):
        for key in za:
            if key[0] == k:
                za[key].wait()
        for n, both in enumerate(multiply(own_a[k], low_a[k], high_a[k], SIDE)):
            if k == 0:
                own_sum[:, tile(n)] = both[0]
            send_sum[k, :, :, tile(n)] = both.astype(jnp.bfloat16)
        for i in range(SIDE):
            dx = (i + k) % SIDE
            if (i, dx) != (0, 0):
                send(
                    send_sum.at[k, i], recv_sum.at[k, i], sum_send.at[k], sum_recv.at[k], peer(i, dx)
                )

    def wait_bytes(ref, sem):
        pltpu.make_async_copy(ref, ref, sem).wait()

    def forward_b(q):
        wait_bytes(own_b.at[q, pl.ds(1, OWNERS - 1)], gather_recv.at[q])
        for way, _, landing, to in ways:
            zb[q, way] = send(
                own_b.at[q], landing.at[q], zb_send.at[way, q], zb_recv.at[way, q], (t, to)
            )

    def part_b(q):
        for way in range(2):
            zb[q, way].wait()
        for n, both in enumerate(multiply(own_b[q], low_b[q], high_b[q], 1)):
            if q == 0:
                total_b[:, tile(n)] = both[0]
            elif q < QUADS - 1:
                total_b[:, tile(n)] += both[0]
            else:
                total = total_b[:, tile(n)] + both[0]
                out_ref[0, BINS:, tile(n)] = total[:BINS]
                out_ref[1, BINS:, tile(n)] = total[BINS:]

    def add_sums(k):
        lowest = 1 if k == 0 else 0
        wait_bytes(recv_sum.at[k, pl.ds(lowest, SIDE - lowest)], sum_recv.at[k])
        total = own_sum[...]
        for i in range(lowest, SIDE):
            total = total + recv_sum[k, i].astype(jnp.float32)
        if k < SIDE - 1:
            own_sum[...] = total
        else:
            out_ref[0, :BINS] = total[:BINS]
            out_ref[1, :BINS] = total[BINS:]

    for k in range(SIDE):
        part_a(k)
        forward_b(k)
    part_b(0)
    part_b(1)
    add_sums(0)
    add_sums(1)
    part_b(2)
    add_sums(2)
    part_b(3)
    add_sums(3)
    for q in range(QUADS):
        wait_bytes(stage_b.at[q, pl.ds(1, OWNERS - 1)], gather_send.at[q])
    for k in range(SIDE):
        lowest = 1 if k == 0 else 0
        wait_bytes(send_sum.at[k, pl.ds(lowest, SIDE - lowest)], sum_send.at[k])


def body(records, pair_list, live_count):
    tables = [jnp.asarray(table) for table in basis_tables()]
    any_space = pl.BlockSpec(memory_space=pl.ANY)
    vmem, bf16, f32 = pltpu.VMEM, jnp.bfloat16, jnp.float32
    dma = pltpu.SemaphoreType.DMA
    block_a = vmem((SIDE, SIDE, SEG, ROWS, CH), bf16)
    block_b = vmem((QUADS, OWNERS, 2, ROWS, CH), bf16)
    return pl.pallas_call(
        kernel,
        out_shape=jax.ShapeDtypeStruct((2, 2 * BINS, PAIRS), f32),
        in_specs=[any_space] * 5,
        out_specs=pl.BlockSpec(memory_space=vmem),
        scratch_shapes=[
            vmem((2, SIDE, SIDE, ROWS, SAMPLES), bf16),
            vmem((SEG, SAMPLES, CH), bf16),
            vmem((2, PAIRS), jnp.int32),
            pltpu.SMEM((1,), jnp.int32),
            vmem((TILES, CH, TILE), bf16),
            vmem((TILES, 3 * CH, TILE), bf16),
            block_a,
            block_a,
            block_a,
            block_b,
            block_b,
            block_b,
            block_b,
            vmem((ROWS, PAIRS), f32),
            vmem((SIDE, SIDE, ROWS, PAIRS), bf16),
            vmem((SIDE, SIDE, ROWS, PAIRS), bf16),
            vmem((ROWS, PAIRS), f32),
            dma((4 + QUADS,)),
            dma((2, QUADS + SIDE - 1)),
            dma((2, QUADS + SIDE - 1)),
            dma((2, QUADS)),
            dma((2, QUADS)),
            dma((QUADS,)),
            dma((QUADS,)),
            dma((SIDE,)),
            dma((SIDE,)),
        ],
        compiler_params=pltpu.CompilerParams(
            collective_id=0, has_side_effects=True, vmem_limit_bytes=56 * 2**20
        ),
        cost_estimate=pl.CostEstimate(
            flops=7 * 10**9, bytes_accessed=4 * 2**20, transcendentals=0
        ),
    )(*tables, records, pair_list, live_count)


def solution(mesh):
    in_specs = (P("tm", None, "chan"), P(None, "chan"), P("chan"))
    out_specs = P(None, "tm", "chan")
    return jax.shard_map(body, mesh=mesh, in_specs=in_specs, out_specs=out_specs, check_vma=False)
```

time: 206 us -> 32.7 us (0.16)
  the two profiles are of different devices: /device:TPU:1 before, /device:TPU:8 now
where the time goes in v2:
time: 32.7 us; the launch traced here: 32.6 us
  Pallas kernels  30.4 us (93%)
  local copies, waits for them, and re-layouts  1.57 us (5%)
  between operations  0.66 us (2%)
    pallas_call x1, Pallas kernels, body(): pl.pallas_call(kernel, out_shape=jax.ShapeDtypeStruct((2, 2 * BINS, PAIRS...  30.4 us
    unnamed x1, local copies, waits for them, and re-layouts  1.57 us

profile of v2, /device:TPU:8, one launch (start us, length us, event | category | flops | bytes accessed | tf_op | source)
XLA Modules:
  0.0 32.6 jit_solution(7781359301363401524)
XLA Ops:
  0.7 30.4 %shard_map.55 = f32[2,16,1024]{2,1,0:T(8,128)} custom-call(bf16[7,7,16,1024]{3,2,1,0:T(8,128)(2,1)} %constant.4.clone.basis_a_hbm, bf16[7,7,16,1024]{3,2,1,0:T(8,128)(2,1)} %constant.5.clone.basis_b_hbm, bf16[8,1024,128]{2,1,0:T(8,128)(2,1)} %rec_hbm.1, s32[2,1024]{1,0:T(2,128)} %pair_hbm.1, s32[1]{0:T(128)S(6)} %copy.7.live_hbm), custom_call_target="tpu_custom_call" | custom-call | flops 7000000000 | bytes 4194304 | tf_op jit(solution)/shard_map/pallas_call | solution.py:242
  31.0 1.6 %copy.8 = f32[2,16,1024]{2,1,0:T(8,128)} copy(f32[2,16,1024]{2,1,0:T(8,128)} %shard_map.55) | data formatting | bytes 262144

commit v3 on v2

--- a/solution.py
+++ b/solution.py
@@ -1,3 +1,4 @@
+import functools
 import math
 
 import jax
@@ -24,6 +25,7 @@
 TILE = 256
 TILES = PAIRS // TILE
 QUADS = SEG // 2
+EARLY = 2
 MESH = pl.DeviceIdType.MESH
 
 
@@ -47,16 +49,24 @@
 def kernel(
     basis_a_hbm, basis_b_hbm, rec_hbm, pair_hbm, live_hbm, out_ref,
     basis, rec, pair, live, w_left, w_right,
-    own_a, low_a, high_a, stage_b, own_b, low_b, high_b, own_sum, send_sum, recv_sum, total_b,
+    own_a, near_a, far_a, stage_b, own_b, near_b, far_b, own_sum, send_sum, recv_sum, total_b,
     in_sem, za_send, za_recv, zb_send, zb_recv, gather_send, gather_recv, sum_send, sum_recv,
 ):
     t = lax.axis_index("tm")
     c = lax.axis_index("chan")
     n_chan = lax.axis_size("chan")
     y, x = lax.div(t, SIDE), lax.rem(t, SIDE)
-    c_high = lax.rem(c + 1, n_chan)
-    c_low = lax.rem(c + n_chan - 1, n_chan)
-    ways = ((0, high_a, high_b, c_low), (1, low_a, low_b, c_high))
+    side = 1 - 2 * lax.rem(c, 2)
+    c_near, c_far = c + side, c - side
+    has_far = jnp.logical_and(c_far >= 0, c_far < n_chan)
+    one_far = jnp.where(has_far, 1, 0)
+    ways = ((0, near_a, near_b, c_near), (1, far_a, far_b, c_far))
+
+    def on_way(way, act):
+        if way == 0:
+            act()
+        else:
+            pl.when(has_far)(act)
 
     def peer(dy, dx):
         return (lax.rem(y + dy, SIDE) * SIDE + lax.rem(x + dx, SIDE), c)
@@ -83,11 +93,20 @@
     live_copy.start()
 
     barrier = pltpu.get_barrier_semaphore()
-    for to in [(t, c_low), (t, c_high)] + [peer(dy, dx) for dy, dx in others]:
+    for to in [(t, c_near)] + [peer(dy, dx) for dy, dx in others]:
         pl.semaphore_signal(barrier, inc=1, device_id=to, device_id_type=MESH)
 
-    def send(source, landing, send_sem, recv_sem, to):
-        copy = pltpu.make_async_remote_copy(
+    @pl.when(has_far)
+    def _():
+        pl.semaphore_signal(barrier, inc=1, device_id=(t, c_far), device_id_type=MESH)
+
+    @pl.when(jnp.logical_not(has_far))
+    def _():
+        far_a[...] = jnp.zeros_like(far_a)
+        far_b[...] = jnp.zeros_like(far_b)
+
+    def make(source, landing, send_sem, recv_sem, to):
+        return pltpu.make_async_remote_copy(
             src_ref=source,
             dst_ref=landing,
             send_sem=send_sem,
@@ -95,10 +114,26 @@
             device_id=to,
             device_id_type=MESH,
         )
-        copy.start()
-        return copy
-
-    za, zb = {}, {}
+
+    za, zb = [], []
+
+    def send_z(copies, started=za):
+        started.extend(copies)
+        for way in (1, 0):
+            @functools.partial(on_way, way)
+            def _():
+                for _, w, copy in copies:
+                    if w == way:
+                        copy.start()
+
+    def wait_z(k, started=za):
+        for way in range(2):
+            @functools.partial(on_way, way)
+            def _():
+                for part, w, copy in started:
+                    if part == k and w == way:
+                        copy.wait()
+
     for copy in basis_copies:
         copy.wait()
     for q in range(QUADS):
@@ -115,23 +150,25 @@
             stage_b[q, :, e] = mine[1]
             own_b[q, 0, e] = mine[1, 0]
         if q == 0:
-            pl.semaphore_wait(barrier, 2 + len(others))
-        piece = (0, pl.ds(0, SIDE), pl.ds(2 * q, 2))
-        for way, landing, _, to in ways:
-            za[0, q, way] = send(
-                own_a.at[piece], landing.at[piece], za_send.at[way, q], za_recv.at[way, q], (t, to)
-            )
+            pl.semaphore_wait(barrier, 1 + one_far + len(others))
+        for k in range(EARLY):
+            piece = (k, pl.ds(0, SIDE), pl.ds(2 * q, 2))
+            sem = k * QUADS + q
+            send_z([
+                (k, way, make(own_a.at[piece], landing.at[piece], za_send.at[way, sem], za_recv.at[way, sem], (t, to)))
+                for way, landing, _, to in ways
+            ])
         for dy, dx in others:
             d = dy * SIDE + dx
-            send(
+            make(
                 stage_b.at[q, d], own_b.at[q, d], gather_send.at[q], gather_recv.at[q], peer(dy, dx)
-            )
-    for k in range(1, SIDE):
-        for way, landing, _, to in ways:
-            sem = QUADS + k - 1
-            za[k, 0, way] = send(
-                own_a.at[k], landing.at[k], za_send.at[way, sem], za_recv.at[way, sem], (t, to)
-            )
+            ).start()
+    for k in range(EARLY, SIDE):
+        sem = QUADS * EARLY + k - EARLY
+        send_z([
+            (k, way, make(own_a.at[k], landing.at[k], za_send.at[way, sem], za_recv.at[way, sem], (t, to)))
+            for way, landing, _, to in ways
+        ])
 
     pair_copy.wait()
     live_copy.wait()
@@ -144,13 +181,13 @@
         left = jnp.where(slots < n_live, left, -1)
         ids = lax.broadcasted_iota(jnp.int32, (CH, TILE), 0)
         w_left[n] = jnp.where(ids == left, 1.0 / 128.0, 0.0).astype(jnp.bfloat16)
-        for place, block in ((0, 1), (1, 0), (2, 2)):
+        for place, block in ((0, 1), (1, 1 + side), (2, 1 - side)):
             hot = jnp.where(ids + block * CH == right, 1.0, 0.0)
             w_right[n, pl.ds(place * CH, CH)] = hot.astype(jnp.bfloat16)
 
-    def multiply(own, low, high, groups):
+    def multiply(own, near, far, groups):
         mine = own.reshape(-1, CH)
-        wide = jnp.concatenate([mine, low.reshape(-1, CH), high.reshape(-1, CH)], axis=1)
+        wide = jnp.concatenate([mine, near.reshape(-1, CH), far.reshape(-1, CH)], axis=1)
         shape = (groups, mine.shape[0] // (groups * ROWS), 2, BINS, TILE)
         sums = []
         for n in range(TILES):
@@ -165,34 +202,31 @@
         return pl.ds(n * TILE, TILE)
 
     def part_a(k):
-        for key in za:
-            if key[0] == k:
-                za[key].wait()
-        for n, both in enumerate(multiply(own_a[k], low_a[k], high_a[k], SIDE)):
+        wait_z(k)
+        for n, both in enumerate(multiply(own_a[k], near_a[k], far_a[k], SIDE)):
             if k == 0:
                 own_sum[:, tile(n)] = both[0]
             send_sum[k, :, :, tile(n)] = both.astype(jnp.bfloat16)
         for i in range(SIDE):
             dx = (i + k) % SIDE
             if (i, dx) != (0, 0):
-                send(
+                make(
                     send_sum.at[k, i], recv_sum.at[k, i], sum_send.at[k], sum_recv.at[k], peer(i, dx)
-                )
+                ).start()
 
     def wait_bytes(ref, sem):
         pltpu.make_async_copy(ref, ref, sem).wait()
 
     def forward_b(q):
         wait_bytes(own_b.at[q, pl.ds(1, OWNERS - 1)], gather_recv.at[q])
-        for way, _, landing, to in ways:
-            zb[q, way] = send(
-                own_b.at[q], landing.at[q], zb_send.at[way, q], zb_recv.at[way, q], (t, to)
-            )
+        send_z([
+            (q, way, make(own_b.at[q], landing.at[q], zb_send.at[way, q], zb_recv.at[way, q], (t, to)))
+            for way, _, landing, to in ways
+        ], zb)
 
     def part_b(q):
-        for way in range(2):
-            zb[q, way].wait()
-        for n, both in enumerate(multiply(own_b[q], low_b[q], high_b[q], 1)):
+        wait_z(q, zb)
+        for n, both in enumerate(multiply(own_b[q], near_b[q], far_b[q], 1)):
             if q == 0:
                 total_b[:, tile(n)] = both[0]
             elif q < QUADS - 1:
@@ -215,8 +249,8 @@
             out_ref[1, :BINS] = total[BINS:]
 
     for k in range(SIDE):
+        forward_b(k)
         part_a(k)
-        forward_b(k)
     part_b(0)
     part_b(1)
     add_sums(0)
@@ -241,7 +275,7 @@
     block_b = vmem((QUADS, OWNERS, 2, ROWS, CH), bf16)
     return pl.pallas_call(
         kernel,
-        out_shape=jax.ShapeDtypeStruct((2, 2 * BINS, PAIRS), f32),
+        out_shape=vmem((2, 2 * BINS, PAIRS), f32),
         in_specs=[any_space] * 5,
         out_specs=pl.BlockSpec(memory_space=vmem),
         scratch_shapes=[
@@ -263,8 +297,8 @@
             vmem((SIDE, SIDE, ROWS, PAIRS), bf16),
             vmem((ROWS, PAIRS), f32),
             dma((4 + QUADS,)),
-            dma((2, QUADS + SIDE - 1)),
-            dma((2, QUADS + SIDE - 1)),
+            dma((2, QUADS * EARLY + SIDE - EARLY)),
+            dma((2, QUADS * EARLY + SIDE - EARLY)),
             dma((2, QUADS)),
             dma((2, QUADS)),
             dma((QUADS,)),

time: 32.7 us -> 26.2 us (0.80)
  the two profiles are of different devices: /device:TPU:8 before, /device:TPU:1 now
where the time goes in v3:
time: 26.2 us; the launch traced here: 26 us
  Pallas kernels  24.6 us (94%)
  local copies, waits for them, and re-layouts  0.66 us (3%)
  between operations  0.66 us (3%)
    pallas_call x1, Pallas kernels, body(): pl.pallas_call(kernel, out_shape=vmem((2, 2 * BINS, PAIRS), f32), in_spec...  24.6 us
    unnamed x1, local copies, waits for them, and re-layouts  0.66 us

profile of v3, /device:TPU:1, one launch (start us, length us, event | category | flops | bytes accessed | tf_op | source)
XLA Modules:
  0.0 26.0 jit_solution(7793901404733558049)
XLA Ops:
  0.7 24.6 %shard_map.55 = f32[2,16,1024]{2,1,0:T(8,128)S(1)} custom-call(bf16[7,7,16,1024]{3,2,1,0:T(8,128)(2,1)} %constant.4.clone.basis_a_hbm, bf16[7,7,16,1024]{3,2,1,0:T(8,128)(2,1)} %constant.5.clone.basis_b_hbm, bf16[8,1024,128]{2,1,0:T(8,128)(2,1)} %rec_hbm.1, s32[2,1024]{1,0:T(2,128)} %pair_hbm.1, s32[1]{0:T(128)S(6)} %copy.8.live_hbm), custom_call_target="tpu_custom_call" | custom-call | flops 7000000000 | bytes 4194304 | tf_op jit(solution)/shard_map/pallas_call | solution.py:276
  25.3 0.7 %copy.7 = f32[2,16,1024]{2,1,0:T(8,128)} copy(f32[2,16,1024]{2,1,0:T(8,128)S(1)} %shard_map.55) | data formatting | bytes 262144

commit v4 on v3

v4 whole, which is shorter than its diff:
```python
import functools
import math

import jax
import jax.numpy as jnp
import ml_dtypes
import numpy as np
from jax import lax
from jax.experimental import pallas as pl
from jax.experimental.pallas import tpu as pltpu
from jax.sharding import PartitionSpec as P

SAMPLES = 1024
NF = 256
BAND_LO = 16
EPSILON = 1e-06

SIDE = 4
SEG = 8
CH = 128
PAIRS = 1024
BINS = 16
ROWS = 2 * BINS
TILE = 256
TILES = PAIRS // TILE
QUADS = SEG // 2
MESH = pl.DeviceIdType.MESH

A_WAY = ((2, 2), (1, 2), (3, 2), (2, 1), (2, 3), (1, 1))
B_WAY = tuple((dy, dx) for dy in range(SIDE) for dx in range(SIDE) if (dy, dx) not in A_WAY)
GROUP = 2
PARTS = len(A_WAY) // GROUP
EARLY = 2


def basis_table():
    sample_ids = np.arange(SAMPLES, dtype=np.int64)
    bin_ids = np.arange(NF, dtype=np.int64) + BAND_LO
    phases = bin_ids[:, None] * sample_ids[None, :] % SAMPLES
    step = np.float32(2.0 * math.pi / SAMPLES)
    angles = phases.astype(np.float32) * step
    tapers = np.float32(0.5) - np.float32(0.5) * np.cos(sample_ids.astype(np.float32) * step)
    table = np.stack([np.cos(angles) * tapers[None, :], -np.sin(angles) * tapers[None, :]])
    table = table.astype(np.float32).astype(ml_dtypes.bfloat16)
    table = table.reshape(2, SIDE, SIDE, BINS, SAMPLES).transpose(1, 2, 0, 3, 4)
    ids = np.arange(2 * SIDE - 1) % SIDE
    return table.reshape(SIDE, SIDE, ROWS, SAMPLES)[ids[:, None], ids[None, :]]


def kernel(
    basis_hbm, rec_hbm, pair_hbm, live_hbm, out_ref,
    basis, rec, pair, live, w_left, w_right,
    own_a, near_a, far_a, stage_b, own_b, near_b, far_b, left_part, right_part, send_sum, recv_sum, total,
    in_sem, za_send, za_recv, zb_send, zb_recv, gather_send, gather_recv, sum_send, sum_recv,
):
    t = lax.axis_index("tm")
    c = lax.axis_index("chan")
    n_chan = lax.axis_size("chan")
    y, x = lax.div(t, SIDE), lax.rem(t, SIDE)
    side = 1 - 2 * lax.rem(c, 2)
    c_near, c_far = c + side, c - side
    has_far = jnp.logical_and(c_far >= 0, c_far < n_chan)
    one_far = jnp.where(has_far, 1, 0)
    ways = ((0, near_a, near_b, c_near), (1, far_a, far_b, c_far))

    def on_way(way, act):
        if way == 0:
            act()
        else:
            pl.when(has_far)(act)

    def peer(dy, dx):
        return (lax.rem(y + dy, SIDE) * SIDE + lax.rem(x + dx, SIDE), c)

    others = [to for to in A_WAY + B_WAY if to != (0, 0)]

    basis_copy = pltpu.make_async_copy(
        basis_hbm.at[pl.ds(y, SIDE), pl.ds(x, SIDE)], basis, in_sem.at[2]
    )
    rec_copies = [
        pltpu.make_async_copy(rec_hbm.at[pl.ds(2 * q, 2)], rec.at[pl.ds(2 * q, 2)], in_sem.at[3 + q])
        for q in range(QUADS)
    ]
    pair_copy = pltpu.make_async_copy(pair_hbm, pair, in_sem.at[0])
    live_copy = pltpu.make_async_copy(live_hbm, live, in_sem.at[1])
    rec_copies[0].start()
    basis_copy.start()
    for q in range(1, QUADS):
        rec_copies[q].start()
    pair_copy.start()
    live_copy.start()

    barrier = pltpu.get_barrier_semaphore()
    for to in [(t, c_near)] + [peer(dy, dx) for dy, dx in others]:
        pl.semaphore_signal(barrier, inc=1, device_id=to, device_id_type=MESH)

    @pl.when(has_far)
    def _():
        pl.semaphore_signal(barrier, inc=1, device_id=(t, c_far), device_id_type=MESH)

    @pl.when(jnp.logical_not(has_far))
    def _():
        far_a[...] = jnp.zeros_like(far_a)
        far_b[...] = jnp.zeros_like(far_b)

    def make(source, landing, send_sem, recv_sem, to):
        return pltpu.make_async_remote_copy(
            src_ref=source,
            dst_ref=landing,
            send_sem=send_sem,
            recv_sem=recv_sem,
            device_id=to,
            device_id_type=MESH,
        )

    za, zb = [], []

    def send_z(copies, started=za):
        started.extend(copies)
        for way in (1, 0):
            @functools.partial(on_way, way)
            def _():
                for _, w, copy in copies:
                    if w == way:
                        copy.start()

    def wait_z(k, way, started=za):
        @functools.partial(on_way, way)
        def _():
            for part, w, copy in started:
                if part == k and w == way:
                    copy.wait()

    basis_copy.wait()
    for q in range(QUADS):
        rec_copies[q].wait()
        wide = jnp.concatenate([rec[2 * q], rec[2 * q + 1]], axis=1)
        spectrum = jnp.dot(
            basis[...].reshape(2 * NF, SAMPLES), wide, preferred_element_type=jnp.float32
        )
        powers = jnp.sum(spectrum * spectrum, axis=0, keepdims=True) / NF
        white = (spectrum * lax.rsqrt(powers + EPSILON)).astype(jnp.bfloat16)
        for e in range(2):
            mine = white[:, e * CH:(e + 1) * CH].reshape(SIDE, SIDE, ROWS, CH)
            for i, (dy, dx) in enumerate(A_WAY):
                own_a[i // GROUP, i % GROUP, 2 * q + e] = mine[dy, dx]
            for i, (dy, dx) in enumerate(B_WAY):
                (own_b if i == 0 else stage_b)[q, i, e] = mine[dy, dx]
        if q == 0:
            pl.semaphore_wait(barrier, 1 + one_far + len(others))
        for k in range(EARLY):
            piece = (k, pl.ds(0, GROUP), pl.ds(2 * q, 2))
            sem = k * QUADS + q
            send_z([
                (k, way, make(own_a.at[piece], landing.at[piece], za_send.at[way, sem], za_recv.at[way, sem], (t, to)))
                for way, landing, _, to in ways
            ])
        for i, to in enumerate(B_WAY):
            if i > 0:
                make(
                    stage_b.at[q, i], own_b.at[q, i], gather_send.at[q], gather_recv.at[q], peer(*to)
                ).start()
    for k in range(EARLY, PARTS):
        sem = QUADS * EARLY + k - EARLY
        send_z([
            (k, way, make(own_a.at[k], landing.at[k], za_send.at[way, sem], za_recv.at[way, sem], (t, to)))
            for way, landing, _, to in ways
        ])

    pair_copy.wait()
    live_copy.wait()
    n_live = live[0]
    for n in range(TILES):
        cols = pl.ds(n * TILE, TILE)
        left = pair[0:1, cols] - c * CH
        right = pair[1:2, cols] - (c - 1) * CH
        slots = lax.broadcasted_iota(jnp.int32, (1, TILE), 1) + n * TILE
        left = jnp.where(slots < n_live, left, -1)
        ids = lax.broadcasted_iota(jnp.int32, (CH, TILE), 0)
        w_left[n] = jnp.where(ids == left, 1.0 / 128.0, 0.0).astype(jnp.bfloat16)
        for place, block in ((0, 1), (1, 1 + side), (2, 1 - side)):
            hot = jnp.where(ids + block * CH == right, 1.0, 0.0)
            w_right[n, pl.ds(place * CH, CH)] = hot.astype(jnp.bfloat16)

    def tile(n):
        return pl.ds(n * TILE, TILE)

    def before(own, near):
        mine = own.reshape(-1, CH)
        rows = pl.ds(0, mine.shape[0])
        wide = jnp.concatenate([mine, near.reshape(-1, CH)], axis=1)
        for n in range(TILES):
            left_part[n, rows] = jnp.dot(mine, w_left[n], preferred_element_type=jnp.float32)
            right_part[n, rows] = jnp.dot(
                wide, w_right[n, :2 * CH], preferred_element_type=jnp.float32
            )

    def after(far, groups):
        far = far.reshape(-1, CH)
        rows = pl.ds(0, far.shape[0])
        shape = (groups, far.shape[0] // (groups * ROWS), 2, BINS, TILE)
        sums = []
        for n in range(TILES):
            left = left_part[n, rows].reshape(shape)
            right = right_part[n, rows] + jnp.dot(
                far, w_right[n, 2 * CH:], preferred_element_type=jnp.float32
            )
            right = right.reshape(shape)
            real = jnp.sum(left[:, :, 0] * right[:, :, 0] + left[:, :, 1] * right[:, :, 1], axis=1)
            imag = jnp.sum(left[:, :, 1] * right[:, :, 0] - left[:, :, 0] * right[:, :, 1], axis=1)
            sums.append(jnp.concatenate([real, imag], axis=1))
        return sums

    def before_a(k):
        wait_z(k, 0)
        before(own_a[k], near_a[k])

    def after_a(k):
        wait_z(k, 1)
        for n, both in enumerate(after(far_a[k], GROUP)):
            send_sum[k, :, :, tile(n)] = both.astype(jnp.bfloat16)
        for i in range(GROUP):
            make(
                send_sum.at[k, i], recv_sum.at[k, i], sum_send.at[k], sum_recv.at[k],
                peer(*A_WAY[k * GROUP + i]),
            ).start()

    def wait_bytes(ref, sem):
        pltpu.make_async_copy(ref, ref, sem).wait()

    def forward_b(q):
        wait_bytes(own_b.at[q, pl.ds(1, len(B_WAY) - 1)], gather_recv.at[q])
        send_z([
            (q, way, make(own_b.at[q], landing.at[q], zb_send.at[way, q], zb_recv.at[way, q], (t, to)))
            for way, _, landing, to in ways
        ], zb)

    def before_b(q):
        wait_z(q, 0, zb)
        before(own_b[q], near_b[q])

    def after_b(q):
        wait_z(q, 1, zb)
        for n, both in enumerate(after(far_b[q], 1)):
            if q == 0:
                total[:, tile(n)] = both[0]
            elif q < QUADS - 1:
                total[:, tile(n)] += both[0]
            else:
                done = total[:, tile(n)] + both[0]
                out_ref[0, :, tile(n)] = done[:BINS]
                out_ref[1, :, tile(n)] = done[BINS:]

    def add_sums(k):
        wait_bytes(recv_sum.at[k], sum_recv.at[k])
        done = total[...]
        for i in range(GROUP):
            done = done + recv_sum[k, i].astype(jnp.float32)
        total[...] = done

    before_a(0)
    after_a(0)
    before_a(1)
    forward_b(0)
    after_a(1)
    forward_b(1)
    before_a(2)
    after_a(2)
    forward_b(2)
    before_b(0)
    forward_b(3)
    after_b(0)
    before_b(1)
    after_b(1)
    add_sums(0)
    before_b(2)
    after_b(2)
    before_b(3)
    add_sums(1)
    add_sums(2)
    after_b(3)
    for q in range(QUADS):
        wait_bytes(stage_b.at[q, pl.ds(1, len(B_WAY) - 1)], gather_send.at[q])
    for k in range(PARTS):
        wait_bytes(send_sum.at[k], sum_send.at[k])


def body(records, pair_list, live_count):
    table = jnp.asarray(basis_table())
    any_space = pl.BlockSpec(memory_space=pl.ANY)
    vmem, bf16, f32 = pltpu.VMEM, jnp.bfloat16, jnp.float32
    dma = pltpu.SemaphoreType.DMA
    block_a = vmem((PARTS, GROUP, SEG, ROWS, CH), bf16)
    block_b = vmem((QUADS, len(B_WAY), 2, ROWS, CH), bf16)
    parts = vmem((TILES, max(GROUP * SEG, 2 * len(B_WAY)) * ROWS, TILE), f32)
    sums = vmem((PARTS, GROUP, ROWS, PAIRS), bf16)
    return pl.pallas_call(
        kernel,
        out_shape=vmem((2, BINS, PAIRS), f32),
        in_specs=[any_space] * 4,
        out_specs=pl.BlockSpec(memory_space=vmem),
        scratch_shapes=[
            vmem((SIDE, SIDE, ROWS, SAMPLES), bf16),
            vmem((SEG, SAMPLES, CH), bf16),
            vmem((2, PAIRS), jnp.int32),
            pltpu.SMEM((1,), jnp.int32),
            vmem((TILES, CH, TILE), bf16),
            vmem((TILES, 3 * CH, TILE), bf16),
            block_a,
            block_a,
            block_a,
            block_b,
            block_b,
            block_b,
            block_b,
            parts,
            parts,
            sums,
            sums,
            vmem((ROWS, PAIRS), f32),
            dma((3 + QUADS,)),
            dma((2, QUADS * EARLY + PARTS - EARLY)),
            dma((2, QUADS * EARLY + PARTS - EARLY)),
            dma((2, QUADS)),
            dma((2, QUADS)),
            dma((QUADS,)),
            dma((QUADS,)),
            dma((PARTS,)),
            dma((PARTS,)),
        ],
        compiler_params=pltpu.CompilerParams(
            collective_id=0, has_side_effects=True, vmem_limit_bytes=56 * 2**20
        ),
        cost_estimate=pl.CostEstimate(
            flops=7 * 10**9, bytes_accessed=4 * 2**20, transcendentals=0
        ),
    )(table, records, pair_list, live_count)


def solution(mesh):
    in_specs = (P("tm", None, "chan"), P(None, "chan"), P("chan"))
    out_specs = P(None, "tm", "chan")
    return jax.shard_map(body, mesh=mesh, in_specs=in_specs, out_specs=out_specs, check_vma=False)
```

time: 26.2 us -> 28.6 us (1.092)
  Pallas kernels: 24.6 us -> 27.1 us
    pallas_call x1, Pallas kernels: 24.6 us -> 27.1 us  [body(): pl.pallas_call(kernel, out_shape=vmem((2, BINS, PAIRS), f32), in_specs=[a...]
where the time goes in v4:
time: 28.6 us; the launch traced here: 28.4 us
  Pallas kernels  27.1 us (95%)
  local copies, waits for them, and re-layouts  0.66 us (2%)
  between operations  0.66 us (2%)
    pallas_call x1, Pallas kernels, body(): pl.pallas_call(kernel, out_shape=vmem((2, BINS, PAIRS), f32), in_specs=[a...  27.1 us
    unnamed x1, local copies, waits for them, and re-layouts  0.66 us

profile of v4, /device:TPU:1, one launch (start us, length us, event | category | flops | bytes accessed | tf_op | source)
XLA Modules:
  0.0 28.4 jit_solution(10688814258605329411)
XLA Ops:
  0.7 27.1 %shard_map.46 = f32[2,16,1024]{2,1,0:T(8,128)S(1)} custom-call(bf16[7,7,32,1024]{3,2,1,0:T(8,128)(2,1)} %constant.2.clone.basis_hbm, bf16[8,1024,128]{2,1,0:T(8,128)(2,1)} %rec_hbm.1, s32[2,1024]{1,0:T(2,128)} %pair_hbm.1, s32[1]{0:T(128)S(6)} %copy.7.live_hbm), custom_call_target="tpu_custom_call" | custom-call | flops 7000000000 | bytes 4194304 | tf_op jit(solution)/shard_map/pallas_call | solution.py:297
  27.8 0.7 %copy.6 = f32[2,16,1024]{2,1,0:T(8,128)} copy(f32[2,16,1024]{2,1,0:T(8,128)S(1)} %shard_map.46) | data formatting | bytes 262144

commit v5 on v4

--- a/solution.py
+++ b/solution.py
@@ -26,10 +26,11 @@
 QUADS = SEG // 2
 MESH = pl.DeviceIdType.MESH
 
-A_WAY = ((2, 2), (1, 2), (3, 2), (2, 1), (2, 3), (1, 1))
+A_WAY = ((2, 2), (1, 2), (3, 2), (2, 1), (2, 3), (0, 0))
 B_WAY = tuple((dy, dx) for dy in range(SIDE) for dx in range(SIDE) if (dy, dx) not in A_WAY)
 GROUP = 2
 PARTS = len(A_WAY) // GROUP
+SENT = tuple(GROUP - (k == PARTS - 1) for k in range(PARTS))
 EARLY = 2
 
 
@@ -145,7 +146,7 @@
             for i, (dy, dx) in enumerate(A_WAY):
                 own_a[i // GROUP, i % GROUP, 2 * q + e] = mine[dy, dx]
             for i, (dy, dx) in enumerate(B_WAY):
-                (own_b if i == 0 else stage_b)[q, i, e] = mine[dy, dx]
+                stage_b[q, i, e] = mine[dy, dx]
         if q == 0:
             pl.semaphore_wait(barrier, 1 + one_far + len(others))
         for k in range(EARLY):
@@ -156,10 +157,9 @@
                 for way, landing, _, to in ways
             ])
         for i, to in enumerate(B_WAY):
-            if i > 0:
-                make(
-                    stage_b.at[q, i], own_b.at[q, i], gather_send.at[q], gather_recv.at[q], peer(*to)
-                ).start()
+            make(
+                stage_b.at[q, i], own_b.at[q, i], gather_send.at[q], gather_recv.at[q], peer(*to)
+            ).start()
     for k in range(EARLY, PARTS):
         sem = QUADS * EARLY + k - EARLY
         send_z([
@@ -218,8 +218,10 @@
     def after_a(k):
         wait_z(k, 1)
         for n, both in enumerate(after(far_a[k], GROUP)):
-            send_sum[k, :, :, tile(n)] = both.astype(jnp.bfloat16)
-        for i in range(GROUP):
+            send_sum[k, :SENT[k], :, tile(n)] = both[:SENT[k]].astype(jnp.bfloat16)
+            if SENT[k] < GROUP:
+                total[:, tile(n)] = both[SENT[k]]
+        for i in range(SENT[k]):
             make(
                 send_sum.at[k, i], recv_sum.at[k, i], sum_send.at[k], sum_recv.at[k],
                 peer(*A_WAY[k * GROUP + i]),
@@ -229,7 +231,7 @@
         pltpu.make_async_copy(ref, ref, sem).wait()
 
     def forward_b(q):
-        wait_bytes(own_b.at[q, pl.ds(1, len(B_WAY) - 1)], gather_recv.at[q])
+        wait_bytes(own_b.at[q], gather_recv.at[q])
         send_z([
             (q, way, make(own_b.at[q], landing.at[q], zb_send.at[way, q], zb_recv.at[way, q], (t, to)))
             for way, _, landing, to in ways
@@ -242,9 +244,7 @@
     def after_b(q):
         wait_z(q, 1, zb)
         for n, both in enumerate(after(far_b[q], 1)):
-            if q == 0:
-                total[:, tile(n)] = both[0]
-            elif q < QUADS - 1:
+            if q < QUADS - 1:
                 total[:, tile(n)] += both[0]
             else:
                 done = total[:, tile(n)] + both[0]
@@ -252,37 +252,32 @@
                 out_ref[1, :, tile(n)] = done[BINS:]
 
     def add_sums(k):
-        wait_bytes(recv_sum.at[k], sum_recv.at[k])
+        wait_bytes(recv_sum.at[k, pl.ds(0, SENT[k])], sum_recv.at[k])
         done = total[...]
-        for i in range(GROUP):
+        for i in range(SENT[k]):
             done = done + recv_sum[k, i].astype(jnp.float32)
         total[...] = done
 
-    before_a(0)
-    after_a(0)
-    before_a(1)
-    forward_b(0)
-    after_a(1)
-    forward_b(1)
-    before_a(2)
-    after_a(2)
-    forward_b(2)
+    for k in range(PARTS):
+        forward_b(k)
+        before_a(k)
+        after_a(k)
+    forward_b(3)
     before_b(0)
-    forward_b(3)
     after_b(0)
     before_b(1)
     after_b(1)
     add_sums(0)
     before_b(2)
     after_b(2)
+    add_sums(1)
     before_b(3)
-    add_sums(1)
     add_sums(2)
     after_b(3)
     for q in range(QUADS):
-        wait_bytes(stage_b.at[q, pl.ds(1, len(B_WAY) - 1)], gather_send.at[q])
+        wait_bytes(stage_b.at[q], gather_send.at[q])
     for k in range(PARTS):
-        wait_bytes(send_sum.at[k], sum_send.at[k])
+        wait_bytes(send_sum.at[k, pl.ds(0, SENT[k])], sum_send.at[k])
 
 
 def body(records, pair_list, live_count):

time: 28.6 us -> 28.4 us (level)
  no operation moved by 1% of the time
where the time goes in v5:
time: 28.4 us; the launch traced here: 28.3 us
  Pallas kernels  27 us (95%)
  local copies, waits for them, and re-layouts  0.66 us (2%)
  between operations  0.66 us (2%)
    pallas_call x1, Pallas kernels, body(): pl.pallas_call(kernel, out_shape=vmem((2, BINS, PAIRS), f32), in_specs=[a...  27 us
    unnamed x1, local copies, waits for them, and re-layouts  0.66 us

profile of v5, /device:TPU:1, one launch (start us, length us, event | category | flops | bytes accessed | tf_op | source)
XLA Modules:
  0.0 28.3 jit_solution(5962498649279610958)
XLA Ops:
  0.7 27.0 %shard_map.46 = f32[2,16,1024]{2,1,0:T(8,128)S(1)} custom-call(bf16[7,7,32,1024]{3,2,1,0:T(8,128)(2,1)} %constant.2.clone.basis_hbm, bf16[8,1024,128]{2,1,0:T(8,128)(2,1)} %rec_hbm.1, s32[2,1024]{1,0:T(2,128)} %pair_hbm.1, s32[1]{0:T(128)S(6)} %copy.7.live_hbm), custom_call_target="tpu_custom_call" | custom-call | flops 7000000000 | bytes 4194304 | tf_op jit(solution)/shard_map/pallas_call | solution.py:292
  27.7 0.7 %copy.6 = f32[2,16,1024]{2,1,0:T(8,128)} copy(f32[2,16,1024]{2,1,0:T(8,128)S(1)} %shard_map.46) | data formatting | bytes 262144

commit v6 on v3

--- a/solution.py
+++ b/solution.py
@@ -25,7 +25,6 @@
 TILE = 256
 TILES = PAIRS // TILE
 QUADS = SEG // 2
-EARLY = 2
 MESH = pl.DeviceIdType.MESH
 
 
@@ -49,7 +48,7 @@
 def kernel(
     basis_a_hbm, basis_b_hbm, rec_hbm, pair_hbm, live_hbm, out_ref,
     basis, rec, pair, live, w_left, w_right,
-    own_a, near_a, far_a, stage_b, own_b, near_b, far_b, own_sum, send_sum, recv_sum, total_b,
+    own_a, near_a, far_a, stage_b, own_b, near_b, far_b, left_part, right_part, own_sum, send_sum, recv_sum, total_b,
     in_sem, za_send, za_recv, zb_send, zb_recv, gather_send, gather_recv, sum_send, sum_recv,
 ):
     t = lax.axis_index("tm")
@@ -126,13 +125,12 @@
                     if w == way:
                         copy.start()
 
-    def wait_z(k, started=za):
-        for way in range(2):
-            @functools.partial(on_way, way)
-            def _():
-                for part, w, copy in started:
-                    if part == k and w == way:
-                        copy.wait()
+    def wait_z(k, way, started=za):
+        @functools.partial(on_way, way)
+        def _():
+            for part, w, copy in started:
+                if part == k and w == way:
+                    copy.wait()
 
     for copy in basis_copies:
         copy.wait()
@@ -149,26 +147,17 @@
             own_a[:, :, 2 * q + e] = mine[0].reshape(SIDE, SIDE, ROWS, CH)
             stage_b[q, :, e] = mine[1]
             own_b[q, 0, e] = mine[1, 0]
-        if q == 0:
-            pl.semaphore_wait(barrier, 1 + one_far + len(others))
-        for k in range(EARLY):
-            piece = (k, pl.ds(0, SIDE), pl.ds(2 * q, 2))
-            sem = k * QUADS + q
-            send_z([
-                (k, way, make(own_a.at[piece], landing.at[piece], za_send.at[way, sem], za_recv.at[way, sem], (t, to)))
-                for way, landing, _, to in ways
-            ])
+    pl.semaphore_wait(barrier, 1 + one_far + len(others))
+    for q in range(QUADS):
+        send_z([
+            (q, way, make(own_a.at[q], landing.at[q], za_send.at[way, q], za_recv.at[way, q], (t, to)))
+            for way, landing, _, to in ways
+        ])
         for dy, dx in others:
             d = dy * SIDE + dx
             make(
                 stage_b.at[q, d], own_b.at[q, d], gather_send.at[q], gather_recv.at[q], peer(dy, dx)
             ).start()
-    for k in range(EARLY, SIDE):
-        sem = QUADS * EARLY + k - EARLY
-        send_z([
-            (k, way, make(own_a.at[k], landing.at[k], za_send.at[way, sem], za_recv.at[way, sem], (t, to)))
-            for way, landing, _, to in ways
-        ])
 
     pair_copy.wait()
     live_copy.wait()
@@ -185,25 +174,38 @@
             hot = jnp.where(ids + block * CH == right, 1.0, 0.0)
             w_right[n, pl.ds(place * CH, CH)] = hot.astype(jnp.bfloat16)
 
-    def multiply(own, near, far, groups):
+    def tile(n):
+        return pl.ds(n * TILE, TILE)
+
+    def before(own, near):
         mine = own.reshape(-1, CH)
-        wide = jnp.concatenate([mine, near.reshape(-1, CH), far.reshape(-1, CH)], axis=1)
-        shape = (groups, mine.shape[0] // (groups * ROWS), 2, BINS, TILE)
+        wide = jnp.concatenate([mine, near.reshape(-1, CH)], axis=1)
+        for n in range(TILES):
+            left_part[n] = jnp.dot(mine, w_left[n], preferred_element_type=jnp.float32)
+            right_part[n] = jnp.dot(wide, w_right[n, :2 * CH], preferred_element_type=jnp.float32)
+
+    def after(far, groups):
+        far = far.reshape(-1, CH)
+        shape = (groups, far.shape[0] // (groups * ROWS), 2, BINS, TILE)
         sums = []
         for n in range(TILES):
-            left = jnp.dot(mine, w_left[n], preferred_element_type=jnp.float32).reshape(shape)
-            right = jnp.dot(wide, w_right[n], preferred_element_type=jnp.float32).reshape(shape)
+            left = left_part[n].reshape(shape)
+            right = right_part[n] + jnp.dot(
+                far, w_right[n, 2 * CH:], preferred_element_type=jnp.float32
+            )
+            right = right.reshape(shape)
             real = jnp.sum(left[:, :, 0] * right[:, :, 0] + left[:, :, 1] * right[:, :, 1], axis=1)
             imag = jnp.sum(left[:, :, 1] * right[:, :, 0] - left[:, :, 0] * right[:, :, 1], axis=1)
             sums.append(jnp.concatenate([real, imag], axis=1))
         return sums
 
-    def tile(n):
-        return pl.ds(n * TILE, TILE)
-
-    def part_a(k):
-        wait_z(k)
-        for n, both in enumerate(multiply(own_a[k], near_a[k], far_a[k], SIDE)):
+    def before_a(k):
+        wait_z(k, 0)
+        before(own_a[k], near_a[k])
+
+    def after_a(k):
+        wait_z(k, 1)
+        for n, both in enumerate(after(far_a[k], SIDE)):
             if k == 0:
                 own_sum[:, tile(n)] = both[0]
             send_sum[k, :, :, tile(n)] = both.astype(jnp.bfloat16)
@@ -224,9 +226,13 @@
             for way, _, landing, to in ways
         ], zb)
 
-    def part_b(q):
-        wait_z(q, zb)
-        for n, both in enumerate(multiply(own_b[q], near_b[q], far_b[q], 1)):
+    def before_b(q):
+        wait_z(q, 0, zb)
+        before(own_b[q], near_b[q])
+
+    def after_b(q):
+        wait_z(q, 1, zb)
+        for n, both in enumerate(after(far_b[q], 1)):
             if q == 0:
                 total_b[:, tile(n)] = both[0]
             elif q < QUADS - 1:
@@ -248,16 +254,29 @@
             out_ref[0, :BINS] = total[:BINS]
             out_ref[1, :BINS] = total[BINS:]
 
-    for k in range(SIDE):
-        forward_b(k)
-        part_a(k)
-    part_b(0)
-    part_b(1)
+    before_a(0)
+    after_a(0)
+    before_a(1)
+    forward_b(0)
+    after_a(1)
+    before_a(2)
+    forward_b(1)
+    after_a(2)
+    before_a(3)
+    after_a(3)
+    forward_b(2)
+    before_b(0)
+    forward_b(3)
+    after_b(0)
+    before_b(1)
+    after_b(1)
     add_sums(0)
+    before_b(2)
+    after_b(2)
     add_sums(1)
-    part_b(2)
+    before_b(3)
     add_sums(2)
-    part_b(3)
+    after_b(3)
     add_sums(3)
     for q in range(QUADS):
         wait_bytes(stage_b.at[q, pl.ds(1, OWNERS - 1)], gather_send.at[q])
@@ -273,6 +292,7 @@
     dma = pltpu.SemaphoreType.DMA
     block_a = vmem((SIDE, SIDE, SEG, ROWS, CH), bf16)
     block_b = vmem((QUADS, OWNERS, 2, ROWS, CH), bf16)
+    parts = vmem((TILES, SIDE * SEG * ROWS, TILE), f32)
     return pl.pallas_call(
         kernel,
         out_shape=vmem((2, 2 * BINS, PAIRS), f32),
@@ -292,13 +312,15 @@
             block_b,
             block_b,
             block_b,
+            parts,
+            parts,
             vmem((ROWS, PAIRS), f32),
             vmem((SIDE, SIDE, ROWS, PAIRS), bf16),
             vmem((SIDE, SIDE, ROWS, PAIRS), bf16),
             vmem((ROWS, PAIRS), f32),
             dma((4 + QUADS,)),
-            dma((2, QUADS * EARLY + SIDE - EARLY)),
-            dma((2, QUADS * EARLY + SIDE - EARLY)),
+            dma((2, SIDE)),
+            dma((2, SIDE)),
             dma((2, QUADS)),
             dma((2, QUADS)),
             dma((QUADS,)),

time: 26.2 us -> 26.6 us (1.015)
  Pallas kernels: 24.6 us -> 25 us
    pallas_call x1, Pallas kernels: 24.6 us -> 25 us  [body(): pl.pallas_call(kernel, out_shape=vmem((2, 2 * BINS, PAIRS), f32), in_spec...]
where the time goes in v6:
time: 26.6 us; the launch traced here: 26.3 us
  Pallas kernels  25 us (94%)
  local copies, waits for them, and re-layouts  0.66 us (2%)
  between operations  0.66 us (2%)
    pallas_call x1, Pallas kernels, body(): pl.pallas_call(kernel, out_shape=vmem((2, 2 * BINS, PAIRS), f32), in_spec...  25 us
    unnamed x1, local copies, waits for them, and re-layouts  0.66 us

profile of v6, /device:TPU:1, one launch (start us, length us, event | category | flops | bytes accessed | tf_op | source)
XLA Modules:
  0.0 26.3 jit_solution(15495201007925180403)
XLA Ops:
  0.7 25.0 %shard_map.55 = f32[2,16,1024]{2,1,0:T(8,128)S(1)} custom-call(bf16[7,7,16,1024]{3,2,1,0:T(8,128)(2,1)} %constant.4.clone.basis_a_hbm, bf16[7,7,16,1024]{3,2,1,0:T(8,128)(2,1)} %constant.5.clone.basis_b_hbm, bf16[8,1024,128]{2,1,0:T(8,128)(2,1)} %rec_hbm.1, s32[2,1024]{1,0:T(2,128)} %pair_hbm.1, s32[1]{0:T(128)S(6)} %copy.8.live_hbm), custom_call_target="tpu_custom_call" | custom-call | flops 7000000000 | bytes 4194304 | tf_op jit(solution)/shard_map/pallas_call | solution.py:296
  25.7 0.7 %copy.7 = f32[2,16,1024]{2,1,0:T(8,128)} copy(f32[2,16,1024]{2,1,0:T(8,128)S(1)} %shard_map.55) | data formatting | bytes 262144

commit v7 on v5

--- a/solution.py
+++ b/solution.py
@@ -16,21 +16,25 @@
 EPSILON = 1e-06
 
 SIDE = 4
+OWNERS = SIDE * SIDE
 SEG = 8
 CH = 128
 PAIRS = 1024
-BINS = 16
+BINS = 8
 ROWS = 2 * BINS
 TILE = 256
 TILES = PAIRS // TILE
 QUADS = SEG // 2
 MESH = pl.DeviceIdType.MESH
 
-A_WAY = ((2, 2), (1, 2), (3, 2), (2, 1), (2, 3), (0, 0))
-B_WAY = tuple((dy, dx) for dy in range(SIDE) for dx in range(SIDE) if (dy, dx) not in A_WAY)
-GROUP = 2
-PARTS = len(A_WAY) // GROUP
-SENT = tuple(GROUP - (k == PARTS - 1) for k in range(PARTS))
+
+PARTS = (
+    ((2, 2), (1, 2), (3, 2), (2, 1)),
+    ((2, 3), (1, 1), (1, 3), (3, 1)),
+    ((3, 3), (0, 2), (2, 0), (0, 1)),
+    ((0, 3), (1, 0), (3, 0), (0, 0)),
+)
+SENT = tuple(sum(to != (0, 0) for to in part) for part in PARTS)
 EARLY = 2
 
 
@@ -43,15 +47,15 @@
     tapers = np.float32(0.5) - np.float32(0.5) * np.cos(sample_ids.astype(np.float32) * step)
     table = np.stack([np.cos(angles) * tapers[None, :], -np.sin(angles) * tapers[None, :]])
     table = table.astype(np.float32).astype(ml_dtypes.bfloat16)
-    table = table.reshape(2, SIDE, SIDE, BINS, SAMPLES).transpose(1, 2, 0, 3, 4)
+    table = table.reshape(2, SIDE, SIDE, 2, BINS, SAMPLES).transpose(1, 2, 3, 0, 4, 5)
     ids = np.arange(2 * SIDE - 1) % SIDE
-    return table.reshape(SIDE, SIDE, ROWS, SAMPLES)[ids[:, None], ids[None, :]]
+    return table.reshape(SIDE, SIDE, 2, ROWS, SAMPLES)[ids[:, None], ids[None, :]]
 
 
 def kernel(
     basis_hbm, rec_hbm, pair_hbm, live_hbm, out_ref,
     basis, rec, pair, live, w_left, w_right,
-    own_a, near_a, far_a, stage_b, own_b, near_b, far_b, left_part, right_part, send_sum, recv_sum, total,
+    own_a, near_a, far_a, stage_b, own_b, near_b, far_b, left_part, right_part, own_sum, send_sum, recv_sum, total_b,
     in_sem, za_send, za_recv, zb_send, zb_recv, gather_send, gather_recv, sum_send, sum_recv,
 ):
     t = lax.axis_index("tm")
@@ -73,7 +77,7 @@
     def peer(dy, dx):
         return (lax.rem(y + dy, SIDE) * SIDE + lax.rem(x + dx, SIDE), c)
 
-    others = [to for to in A_WAY + B_WAY if to != (0, 0)]
+    others = [to for part in PARTS for to in part if to != (0, 0)]
 
     basis_copy = pltpu.make_async_copy(
         basis_hbm.at[pl.ds(y, SIDE), pl.ds(x, SIDE)], basis, in_sem.at[2]
@@ -86,18 +90,19 @@
     live_copy = pltpu.make_async_copy(live_hbm, live, in_sem.at[1])
     rec_copies[0].start()
     basis_copy.start()
+
+    barrier = pltpu.get_barrier_semaphore()
+    for to in [(t, c_near)] + [peer(dy, dx) for dy, dx in others]:
+        pl.semaphore_signal(barrier, inc=1, device_id=to, device_id_type=MESH)
+
+    @pl.when(has_far)
+    def _():
+        pl.semaphore_signal(barrier, inc=1, device_id=(t, c_far), device_id_type=MESH)
+
     for q in range(1, QUADS):
         rec_copies[q].start()
     pair_copy.start()
     live_copy.start()
-
-    barrier = pltpu.get_barrier_semaphore()
-    for to in [(t, c_near)] + [peer(dy, dx) for dy, dx in others]:
-        pl.semaphore_signal(barrier, inc=1, device_id=to, device_id_type=MESH)
-
-    @pl.when(has_far)
-    def _():
-        pl.semaphore_signal(barrier, inc=1, device_id=(t, c_far), device_id_type=MESH)
 
     @pl.when(jnp.logical_not(has_far))
     def _():
@@ -142,25 +147,27 @@
         powers = jnp.sum(spectrum * spectrum, axis=0, keepdims=True) / NF
         white = (spectrum * lax.rsqrt(powers + EPSILON)).astype(jnp.bfloat16)
         for e in range(2):
-            mine = white[:, e * CH:(e + 1) * CH].reshape(SIDE, SIDE, ROWS, CH)
-            for i, (dy, dx) in enumerate(A_WAY):
-                own_a[i // GROUP, i % GROUP, 2 * q + e] = mine[dy, dx]
-            for i, (dy, dx) in enumerate(B_WAY):
-                stage_b[q, i, e] = mine[dy, dx]
+            mine = white[:, e * CH:(e + 1) * CH].reshape(SIDE, SIDE, 2, ROWS, CH)
+            for k, part in enumerate(PARTS):
+                for i, (dy, dx) in enumerate(part):
+                    own_a[k, i, 2 * q + e] = mine[dy, dx, 0]
+            stage_b[q, :, e] = mine[:, :, 1].reshape(OWNERS, ROWS, CH)
+            own_b[q, 0, e] = mine[0, 0, 1]
         if q == 0:
             pl.semaphore_wait(barrier, 1 + one_far + len(others))
         for k in range(EARLY):
-            piece = (k, pl.ds(0, GROUP), pl.ds(2 * q, 2))
+            piece = (k, pl.ds(0, SIDE), pl.ds(2 * q, 2))
             sem = k * QUADS + q
             send_z([
                 (k, way, make(own_a.at[piece], landing.at[piece], za_send.at[way, sem], za_recv.at[way, sem], (t, to)))
                 for way, landing, _, to in ways
             ])
-        for i, to in enumerate(B_WAY):
+        for dy, dx in others:
+            d = dy * SIDE + dx
             make(
-                stage_b.at[q, i], own_b.at[q, i], gather_send.at[q], gather_recv.at[q], peer(*to)
+                stage_b.at[q, d], own_b.at[q, d], gather_send.at[q], gather_recv.at[q], peer(dy, dx)
             ).start()
-    for k in range(EARLY, PARTS):
+    for k in range(EARLY, SIDE):
         sem = QUADS * EARLY + k - EARLY
         send_z([
             (k, way, make(own_a.at[k], landing.at[k], za_send.at[way, sem], za_recv.at[way, sem], (t, to)))
@@ -187,22 +194,18 @@
 
     def before(own, near):
         mine = own.reshape(-1, CH)
-        rows = pl.ds(0, mine.shape[0])
         wide = jnp.concatenate([mine, near.reshape(-1, CH)], axis=1)
         for n in range(TILES):
-            left_part[n, rows] = jnp.dot(mine, w_left[n], preferred_element_type=jnp.float32)
-            right_part[n, rows] = jnp.dot(
-                wide, w_right[n, :2 * CH], preferred_element_type=jnp.float32
-            )
+            left_part[n] = jnp.dot(mine, w_left[n], preferred_element_type=jnp.float32)
+            right_part[n] = jnp.dot(wide, w_right[n, :2 * CH], preferred_element_type=jnp.float32)
 
     def after(far, groups):
         far = far.reshape(-1, CH)
-        rows = pl.ds(0, far.shape[0])
         shape = (groups, far.shape[0] // (groups * ROWS), 2, BINS, TILE)
         sums = []
         for n in range(TILES):
-            left = left_part[n, rows].reshape(shape)
-            right = right_part[n, rows] + jnp.dot(
+            left = left_part[n].reshape(shape)
+            right = right_part[n] + jnp.dot(
                 far, w_right[n, 2 * CH:], preferred_element_type=jnp.float32
             )
             right = right.reshape(shape)
@@ -217,21 +220,20 @@
 
     def after_a(k):
         wait_z(k, 1)
-        for n, both in enumerate(after(far_a[k], GROUP)):
+        for n, both in enumerate(after(far_a[k], SIDE)):
             send_sum[k, :SENT[k], :, tile(n)] = both[:SENT[k]].astype(jnp.bfloat16)
-            if SENT[k] < GROUP:
-                total[:, tile(n)] = both[SENT[k]]
+            if SENT[k] < SIDE:
+                own_sum[:, tile(n)] = both[SENT[k]]
         for i in range(SENT[k]):
             make(
-                send_sum.at[k, i], recv_sum.at[k, i], sum_send.at[k], sum_recv.at[k],
-                peer(*A_WAY[k * GROUP + i]),
+                send_sum.at[k, i], recv_sum.at[k, i], sum_send.at[k], sum_recv.at[k], peer(*PARTS[k][i])
             ).start()
 
     def wait_bytes(ref, sem):
         pltpu.make_async_copy(ref, ref, sem).wait()
 
     def forward_b(q):
-        wait_bytes(own_b.at[q], gather_recv.at[q])
+        wait_bytes(own_b.at[q, pl.ds(1, OWNERS - 1)], gather_recv.at[q])
         send_z([
             (q, way, make(own_b.at[q], landing.at[q], zb_send.at[way, q], zb_recv.at[way, q], (t, to)))
             for way, _, landing, to in ways
@@ -244,39 +246,45 @@
     def after_b(q):
         wait_z(q, 1, zb)
         for n, both in enumerate(after(far_b[q], 1)):
-            if q < QUADS - 1:
-                total[:, tile(n)] += both[0]
+            if q == 0:
+                total_b[:, tile(n)] = both[0]
+            elif q < QUADS - 1:
+                total_b[:, tile(n)] += both[0]
             else:
-                done = total[:, tile(n)] + both[0]
-                out_ref[0, :, tile(n)] = done[:BINS]
-                out_ref[1, :, tile(n)] = done[BINS:]
+                total = total_b[:, tile(n)] + both[0]
+                out_ref[0, BINS:, tile(n)] = total[:BINS]
+                out_ref[1, BINS:, tile(n)] = total[BINS:]
 
     def add_sums(k):
         wait_bytes(recv_sum.at[k, pl.ds(0, SENT[k])], sum_recv.at[k])
-        done = total[...]
+        total = own_sum[...]
         for i in range(SENT[k]):
-            done = done + recv_sum[k, i].astype(jnp.float32)
-        total[...] = done
-
-    for k in range(PARTS):
+            total = total + recv_sum[k, i].astype(jnp.float32)
+        if k < SIDE - 1:
+            own_sum[...] = total
+        else:
+            out_ref[0, :BINS] = total[:BINS]
+            out_ref[1, :BINS] = total[BINS:]
+
+    for k in range(SIDE):
         forward_b(k)
         before_a(k)
         after_a(k)
-    forward_b(3)
     before_b(0)
     after_b(0)
     before_b(1)
     after_b(1)
     add_sums(0)
+    add_sums(1)
     before_b(2)
     after_b(2)
-    add_sums(1)
+    add_sums(2)
     before_b(3)
-    add_sums(2)
+    add_sums(3)
     after_b(3)
     for q in range(QUADS):
-        wait_bytes(stage_b.at[q], gather_send.at[q])
-    for k in range(PARTS):
+        wait_bytes(stage_b.at[q, pl.ds(1, OWNERS - 1)], gather_send.at[q])
+    for k in range(SIDE):
         wait_bytes(send_sum.at[k, pl.ds(0, SENT[k])], sum_send.at[k])
 
 
@@ -285,17 +293,16 @@
     any_space = pl.BlockSpec(memory_space=pl.ANY)
     vmem, bf16, f32 = pltpu.VMEM, jnp.bfloat16, jnp.float32
     dma = pltpu.SemaphoreType.DMA
-    block_a = vmem((PARTS, GROUP, SEG, ROWS, CH), bf16)
-    block_b = vmem((QUADS, len(B_WAY), 2, ROWS, CH), bf16)
-    parts = vmem((TILES, max(GROUP * SEG, 2 * len(B_WAY)) * ROWS, TILE), f32)
-    sums = vmem((PARTS, GROUP, ROWS, PAIRS), bf16)
+    block_a = vmem((SIDE, SIDE, SEG, ROWS, CH), bf16)
+    block_b = vmem((QUADS, OWNERS, 2, ROWS, CH), bf16)
+    parts = vmem((TILES, SIDE * SEG * ROWS, TILE), f32)
     return pl.pallas_call(
         kernel,
-        out_shape=vmem((2, BINS, PAIRS), f32),
+        out_shape=vmem((2, 2 * BINS, PAIRS), f32),
         in_specs=[any_space] * 4,
         out_specs=pl.BlockSpec(memory_space=vmem),
         scratch_shapes=[
-            vmem((SIDE, SIDE, ROWS, SAMPLES), bf16),
+            vmem((SIDE, SIDE, 2, ROWS, SAMPLES), bf16),
             vmem((SEG, SAMPLES, CH), bf16),
             vmem((2, PAIRS), jnp.int32),
             pltpu.SMEM((1,), jnp.int32),
@@ -310,18 +317,19 @@
             block_b,
             parts,
             parts,
-            sums,
-            sums,
+            vmem((ROWS, PAIRS), f32),
+            vmem((SIDE, SIDE, ROWS, PAIRS), bf16),
+            vmem((SIDE, SIDE, ROWS, PAIRS), bf16),
             vmem((ROWS, PAIRS), f32),
             dma((3 + QUADS,)),
-            dma((2, QUADS * EARLY + PARTS - EARLY)),
-            dma((2, QUADS * EARLY + PARTS - EARLY)),
+            dma((2, QUADS * EARLY + SIDE - EARLY)),
+            dma((2, QUADS * EARLY + SIDE - EARLY)),
             dma((2, QUADS)),
             dma((2, QUADS)),
             dma((QUADS,)),
             dma((QUADS,)),
-            dma((PARTS,)),
-            dma((PARTS,)),
+            dma((SIDE,)),
+            dma((SIDE,)),
         ],
         compiler_params=pltpu.CompilerParams(
             collective_id=0, has_side_effects=True, vmem_limit_bytes=56 * 2**20

time: 28.4 us -> 27.3 us (0.961)
  Pallas kernels: 27 us -> 25.8 us
    pallas_call x1, Pallas kernels: 27 us -> 25.8 us  [body(): pl.pallas_call(kernel, out_shape=vmem((2, 2 * BINS, PAIRS), f32), in_spec...]
where the time goes in v7:
time: 27.3 us; the launch traced here: 27.2 us
  Pallas kernels  25.8 us (95%)
  local copies, waits for them, and re-layouts  0.66 us (2%)
  between operations  0.66 us (2%)
    pallas_call x1, Pallas kernels, body(): pl.pallas_call(kernel, out_shape=vmem((2, 2 * BINS, PAIRS), f32), in_spec...  25.8 us
    unnamed x1, local copies, waits for them, and re-layouts  0.66 us

profile of v7, /device:TPU:1, one launch (start us, length us, event | category | flops | bytes accessed | tf_op | source)
XLA Modules:
  0.0 27.2 jit_solution(2804707070935417849)
XLA Ops:
  0.7 25.8 %shard_map.46 = f32[2,16,1024]{2,1,0:T(8,128)S(1)} custom-call(bf16[7,7,2,16,1024]{4,3,2,1,0:T(8,128)(2,1)} %constant.2.clone.basis_hbm, bf16[8,1024,128]{2,1,0:T(8,128)(2,1)} %rec_hbm.1, s32[2,1024]{1,0:T(2,128)} %pair_hbm.1, s32[1]{0:T(128)S(6)} %copy.7.live_hbm), custom_call_target="tpu_custom_call" | custom-call | flops 7000000000 | bytes 4194304 | tf_op jit(solution)/shard_map/pallas_call | solution.py:299
  26.5 0.7 %copy.6 = f32[2,16,1024]{2,1,0:T(8,128)} copy(f32[2,16,1024]{2,1,0:T(8,128)S(1)} %shard_map.46) | data formatting | bytes 262144

commit v8 on v6

--- a/solution.py
+++ b/solution.py
@@ -25,6 +25,7 @@
 TILE = 256
 TILES = PAIRS // TILE
 QUADS = SEG // 2
+EARLY = 2
 MESH = pl.DeviceIdType.MESH
 
 
@@ -147,17 +148,26 @@
             own_a[:, :, 2 * q + e] = mine[0].reshape(SIDE, SIDE, ROWS, CH)
             stage_b[q, :, e] = mine[1]
             own_b[q, 0, e] = mine[1, 0]
-    pl.semaphore_wait(barrier, 1 + one_far + len(others))
-    for q in range(QUADS):
-        send_z([
-            (q, way, make(own_a.at[q], landing.at[q], za_send.at[way, q], za_recv.at[way, q], (t, to)))
-            for way, landing, _, to in ways
-        ])
+        if q == 0:
+            pl.semaphore_wait(barrier, 1 + one_far + len(others))
+        for k in range(EARLY):
+            piece = (k, pl.ds(0, SIDE), pl.ds(2 * q, 2))
+            sem = k * QUADS + q
+            send_z([
+                (k, way, make(own_a.at[piece], landing.at[piece], za_send.at[way, sem], za_recv.at[way, sem], (t, to)))
+                for way, landing, _, to in ways
+            ])
         for dy, dx in others:
             d = dy * SIDE + dx
             make(
                 stage_b.at[q, d], own_b.at[q, d], gather_send.at[q], gather_recv.at[q], peer(dy, dx)
             ).start()
+    for k in range(EARLY, SIDE):
+        sem = QUADS * EARLY + k - EARLY
+        send_z([
+            (k, way, make(own_a.at[k], landing.at[k], za_send.at[way, sem], za_recv.at[way, sem], (t, to)))
+            for way, landing, _, to in ways
+        ])
 
     pair_copy.wait()
     live_copy.wait()
@@ -263,8 +273,8 @@
     forward_b(1)
     after_a(2)
     before_a(3)
+    forward_b(2)
     after_a(3)
-    forward_b(2)
     before_b(0)
     forward_b(3)
     after_b(0)
@@ -319,8 +329,8 @@
             vmem((SIDE, SIDE, ROWS, PAIRS), bf16),
             vmem((ROWS, PAIRS), f32),
             dma((4 + QUADS,)),
-            dma((2, SIDE)),
-            dma((2, SIDE)),
+            dma((2, QUADS * EARLY + SIDE - EARLY)),
+            dma((2, QUADS * EARLY + SIDE - EARLY)),
             dma((2, QUADS)),
             dma((2, QUADS)),
             dma((QUADS,)),

time: 26.6 us -> 27 us (1.015)
  no operation moved by 1% of the time
where the time goes in v8:
time: 27 us; the launch traced here: 26.5 us
  Pallas kernels  25.2 us (93%)
  local copies, waits for them, and re-layouts  0.66 us (2%)
  between operations  0.66 us (2%)
    pallas_call x1, Pallas kernels, body(): pl.pallas_call(kernel, out_shape=vmem((2, 2 * BINS, PAIRS), f32), in_spec...  25.2 us
    unnamed x1, local copies, waits for them, and re-layouts  0.66 us

profile of v8, /device:TPU:1, one launch (start us, length us, event | category | flops | bytes accessed | tf_op | source)
XLA Modules:
  0.0 26.5 jit_solution(10187628527901666020)
XLA Ops:
  0.7 25.2 %shard_map.55 = f32[2,16,1024]{2,1,0:T(8,128)S(1)} custom-call(bf16[7,7,16,1024]{3,2,1,0:T(8,128)(2,1)} %constant.4.clone.basis_a_hbm, bf16[7,7,16,1024]{3,2,1,0:T(8,128)(2,1)} %constant.5.clone.basis_b_hbm, bf16[8,1024,128]{2,1,0:T(8,128)(2,1)} %rec_hbm.1, s32[2,1024]{1,0:T(2,128)} %pair_hbm.1, s32[1]{0:T(128)S(6)} %copy.8.live_hbm), custom_call_target="tpu_custom_call" | custom-call | flops 7000000000 | bytes 4194304 | tf_op jit(solution)/shard_map/pallas_call | solution.py:306
  25.9 0.7 %copy.7 = f32[2,16,1024]{2,1,0:T(8,128)} copy(f32[2,16,1024]{2,1,0:T(8,128)S(1)} %shard_map.55) | data formatting | bytes 262144

commit v9 on v8

--- a/solution.py
+++ b/solution.py
@@ -72,6 +72,14 @@
         return (lax.rem(y + dy, SIDE) * SIDE + lax.rem(x + dx, SIDE), c)
 
     others = [(dy, dx) for dy in (2, 1, 3, 0) for dx in (2, 1, 3, 0) if (dy, dx) != (0, 0)]
+
+    barrier = pltpu.get_barrier_semaphore()
+    for to in [peer(dy, dx) for dy, dx in others] + [(t, c_near)]:
+        pl.semaphore_signal(barrier, inc=1, device_id=to, device_id_type=MESH)
+
+    @pl.when(has_far)
+    def _():
+        pl.semaphore_signal(barrier, inc=1, device_id=(t, c_far), device_id_type=MESH)
 
     skew = lax.rem(x - y + SIDE, SIDE)
     basis_copies = [
@@ -92,14 +100,6 @@
     pair_copy.start()
     live_copy.start()
 
-    barrier = pltpu.get_barrier_semaphore()
-    for to in [(t, c_near)] + [peer(dy, dx) for dy, dx in others]:
-        pl.semaphore_signal(barrier, inc=1, device_id=to, device_id_type=MESH)
-
-    @pl.when(has_far)
-    def _():
-        pl.semaphore_signal(barrier, inc=1, device_id=(t, c_far), device_id_type=MESH)
-
     @pl.when(jnp.logical_not(has_far))
     def _():
         far_a[...] = jnp.zeros_like(far_a)
@@ -149,19 +149,23 @@
             stage_b[q, :, e] = mine[1]
             own_b[q, 0, e] = mine[1, 0]
         if q == 0:
+            continue
+        if q == 1:
             pl.semaphore_wait(barrier, 1 + one_far + len(others))
+        ready = (0, 1) if q == 1 else (q,)
         for k in range(EARLY):
-            piece = (k, pl.ds(0, SIDE), pl.ds(2 * q, 2))
+            piece = (k, pl.ds(0, SIDE), pl.ds(2 * ready[0], 2 * len(ready)))
             sem = k * QUADS + q
             send_z([
                 (k, way, make(own_a.at[piece], landing.at[piece], za_send.at[way, sem], za_recv.at[way, sem], (t, to)))
                 for way, landing, _, to in ways
             ])
-        for dy, dx in others:
-            d = dy * SIDE + dx
-            make(
-                stage_b.at[q, d], own_b.at[q, d], gather_send.at[q], gather_recv.at[q], peer(dy, dx)
-            ).start()
+        for p in ready:
+            for dy, dx in others:
+                d = dy * SIDE + dx
+                make(
+                    stage_b.at[p, d], own_b.at[p, d], gather_send.at[p], gather_recv.at[p], peer(dy, dx)
+                ).start()
     for k in range(EARLY, SIDE):
         sem = QUADS * EARLY + k - EARLY
         send_z([

time: 27 us -> 26.6 us (0.985); the launches traced: 26.5 us -> 26.5 us
  no operation moved by 1% of the time
where the time goes in v9:
time: 26.6 us; the launch traced here: 26.5 us
  Pallas kernels  25.1 us (94%)
  local copies, waits for them, and re-layouts  0.66 us (2%)
  between operations  0.66 us (2%)
    pallas_call x1, Pallas kernels, body(): pl.pallas_call(kernel, out_shape=vmem((2, 2 * BINS, PAIRS), f32), in_spec...  25.1 us
    unnamed x1, local copies, waits for them, and re-layouts  0.66 us

profile of v9, /device:TPU:1, one launch (start us, length us, event | category | flops | bytes accessed | tf_op | source)
XLA Modules:
  0.0 26.5 jit_solution(527702718254726068)
XLA Ops:
  0.7 25.1 %shard_map.55 = f32[2,16,1024]{2,1,0:T(8,128)S(1)} custom-call(bf16[7,7,16,1024]{3,2,1,0:T(8,128)(2,1)} %constant.4.clone.basis_a_hbm, bf16[7,7,16,1024]{3,2,1,0:T(8,128)(2,1)} %constant.5.clone.basis_b_hbm, bf16[8,1024,128]{2,1,0:T(8,128)(2,1)} %rec_hbm.1, s32[2,1024]{1,0:T(2,128)} %pair_hbm.1, s32[1]{0:T(128)S(6)} %copy.8.live_hbm), custom_call_target="tpu_custom_call" | custom-call | flops 7000000000 | bytes 4194304 | tf_op jit(solution)/shard_map/pallas_call | solution.py:310
  25.8 0.7 %copy.7 = f32[2,16,1024]{2,1,0:T(8,128)} copy(f32[2,16,1024]{2,1,0:T(8,128)S(1)} %shard_map.55) | data formatting | bytes 262144

commit v10 on v9

--- a/solution.py
+++ b/solution.py
@@ -268,19 +268,14 @@
             out_ref[0, :BINS] = total[:BINS]
             out_ref[1, :BINS] = total[BINS:]
 
-    before_a(0)
-    after_a(0)
-    before_a(1)
-    forward_b(0)
-    after_a(1)
-    before_a(2)
-    forward_b(1)
-    after_a(2)
-    before_a(3)
-    forward_b(2)
-    after_a(3)
+    for k in range(SIDE - 1):
+        forward_b(k)
+        before_a(k)
+        after_a(k)
+    before_a(SIDE - 1)
+    after_a(SIDE - 1)
+    forward_b(SIDE - 1)
     before_b(0)
-    forward_b(3)
     after_b(0)
     before_b(1)
     after_b(1)

time: 26.6 us -> 26.6 us (level)
  no operation moved by 1% of the time
where the time goes in v10:
time: 26.6 us; the launch traced here: 26.5 us
  Pallas kernels  25.2 us (95%)
  local copies, waits for them, and re-layouts  0.66 us (2%)
  between operations  0.66 us (2%)
    pallas_call x1, Pallas kernels, body(): pl.pallas_call(kernel, out_shape=vmem((2, 2 * BINS, PAIRS), f32), in_spec...  25.2 us
    unnamed x1, local copies, waits for them, and re-layouts  0.66 us

profile of v10, /device:TPU:1, one launch (start us, length us, event | category | flops | bytes accessed | tf_op | source)
XLA Modules:
  0.0 26.5 jit_solution(4323228910265645277)
XLA Ops:
  0.7 25.2 %shard_map.55 = f32[2,16,1024]{2,1,0:T(8,128)S(1)} custom-call(bf16[7,7,16,1024]{3,2,1,0:T(8,128)(2,1)} %constant.4.clone.basis_a_hbm, bf16[7,7,16,1024]{3,2,1,0:T(8,128)(2,1)} %constant.5.clone.basis_b_hbm, bf16[8,1024,128]{2,1,0:T(8,128)(2,1)} %rec_hbm.1, s32[2,1024]{1,0:T(2,128)} %pair_hbm.1, s32[1]{0:T(128)S(6)} %copy.8.live_hbm), custom_call_target="tpu_custom_call" | custom-call | flops 7000000000 | bytes 4194304 | tf_op jit(solution)/shard_map/pallas_call | solution.py:305
  25.8 0.7 %copy.7 = f32[2,16,1024]{2,1,0:T(8,128)} copy(f32[2,16,1024]{2,1,0:T(8,128)S(1)} %shard_map.55) | data formatting | bytes 262144

commit v11 on v9

--- a/solution.py
+++ b/solution.py
@@ -26,6 +26,9 @@
 TILES = PAIRS // TILE
 QUADS = SEG // 2
 EARLY = 2
+PIECES = tuple((q, 0, OWNERS) for q in range(QUADS - 1)) + tuple(
+    (QUADS - 1, h * OWNERS // 2, OWNERS // 2) for h in range(2)
+)
 MESH = pl.DeviceIdType.MESH
 
 
@@ -194,17 +197,21 @@
     def before(own, near):
         mine = own.reshape(-1, CH)
         wide = jnp.concatenate([mine, near.reshape(-1, CH)], axis=1)
+        rows = pl.ds(0, mine.shape[0])
         for n in range(TILES):
-            left_part[n] = jnp.dot(mine, w_left[n], preferred_element_type=jnp.float32)
-            right_part[n] = jnp.dot(wide, w_right[n, :2 * CH], preferred_element_type=jnp.float32)
+            left_part[n, rows] = jnp.dot(mine, w_left[n], preferred_element_type=jnp.float32)
+            right_part[n, rows] = jnp.dot(
+                wide, w_right[n, :2 * CH], preferred_element_type=jnp.float32
+            )
 
     def after(far, groups):
         far = far.reshape(-1, CH)
+        rows = pl.ds(0, far.shape[0])
         shape = (groups, far.shape[0] // (groups * ROWS), 2, BINS, TILE)
         sums = []
         for n in range(TILES):
-            left = left_part[n].reshape(shape)
-            right = right_part[n] + jnp.dot(
+            left = left_part[n, rows].reshape(shape)
+            right = right_part[n, rows] + jnp.dot(
                 far, w_right[n, 2 * CH:], preferred_element_type=jnp.float32
             )
             right = right.reshape(shape)
@@ -235,21 +242,26 @@
 
     def forward_b(q):
         wait_bytes(own_b.at[q, pl.ds(1, OWNERS - 1)], gather_recv.at[q])
-        send_z([
-            (q, way, make(own_b.at[q], landing.at[q], zb_send.at[way, q], zb_recv.at[way, q], (t, to)))
-            for way, _, landing, to in ways
-        ], zb)
-
-    def before_b(q):
-        wait_z(q, 0, zb)
-        before(own_b[q], near_b[q])
-
-    def after_b(q):
-        wait_z(q, 1, zb)
-        for n, both in enumerate(after(far_b[q], 1)):
-            if q == 0:
+        for p, (pair_id, source, count) in enumerate(PIECES):
+            if pair_id == q:
+                piece = (q, pl.ds(source, count))
+                send_z([
+                    (p, way, make(own_b.at[piece], landing.at[piece], zb_send.at[way, p], zb_recv.at[way, p], (t, to)))
+                    for way, _, landing, to in ways
+                ], zb)
+
+    def before_b(p):
+        wait_z(p, 0, zb)
+        q, source, count = PIECES[p]
+        before(own_b[q, source:source + count], near_b[q, source:source + count])
+
+    def after_b(p):
+        wait_z(p, 1, zb)
+        q, source, count = PIECES[p]
+        for n, both in enumerate(after(far_b[q, source:source + count], 1)):
+            if p == 0:
                 total_b[:, tile(n)] = both[0]
-            elif q < QUADS - 1:
+            elif p < len(PIECES) - 1:
                 total_b[:, tile(n)] += both[0]
             else:
                 total = total_b[:, tile(n)] + both[0]
@@ -291,6 +303,8 @@
     before_b(3)
     add_sums(2)
     after_b(3)
+    before_b(4)
+    after_b(4)
     add_sums(3)
     for q in range(QUADS):
         wait_bytes(stage_b.at[q, pl.ds(1, OWNERS - 1)], gather_send.at[q])
@@ -335,8 +349,8 @@
             dma((4 + QUADS,)),
             dma((2, QUADS * EARLY + SIDE - EARLY)),
             dma((2, QUADS * EARLY + SIDE - EARLY)),
-            dma((2, QUADS)),
-            dma((2, QUADS)),
+            dma((2, len(PIECES))),
+            dma((2, len(PIECES))),
             dma((QUADS,)),
             dma((QUADS,)),
             dma((SIDE,)),

time: 26.6 us -> 27 us (1.015)
  Pallas kernels: 25.1 us -> 25.5 us
    pallas_call x1, Pallas kernels: 25.1 us -> 25.5 us  [body(): pl.pallas_call(kernel, out_shape=vmem((2, 2 * BINS, PAIRS), f32), in_spec...]
where the time goes in v11:
time: 27 us; the launch traced here: 26.8 us
  Pallas kernels  25.5 us (94%)
  local copies, waits for them, and re-layouts  0.66 us (2%)
  between operations  0.66 us (2%)
    pallas_call x1, Pallas kernels, body(): pl.pallas_call(kernel, out_shape=vmem((2, 2 * BINS, PAIRS), f32), in_spec...  25.5 us
    unnamed x1, local copies, waits for them, and re-layouts  0.66 us

profile of v11, /device:TPU:1, one launch (start us, length us, event | category | flops | bytes accessed | tf_op | source)
XLA Modules:
  0.0 26.8 jit_solution(13734947143891588399)
XLA Ops:
  0.7 25.5 %shard_map.55 = f32[2,16,1024]{2,1,0:T(8,128)S(1)} custom-call(bf16[7,7,16,1024]{3,2,1,0:T(8,128)(2,1)} %constant.4.clone.basis_a_hbm, bf16[7,7,16,1024]{3,2,1,0:T(8,128)(2,1)} %constant.5.clone.basis_b_hbm, bf16[8,1024,128]{2,1,0:T(8,128)(2,1)} %rec_hbm.1, s32[2,1024]{1,0:T(2,128)} %pair_hbm.1, s32[1]{0:T(128)S(6)} %copy.8.live_hbm), custom_call_target="tpu_custom_call" | custom-call | flops 7000000000 | bytes 4194304 | tf_op jit(solution)/shard_map/pallas_call | solution.py:324
  26.2 0.7 %copy.7 = f32[2,16,1024]{2,1,0:T(8,128)} copy(f32[2,16,1024]{2,1,0:T(8,128)S(1)} %shard_map.55) | data formatting | bytes 262144

commit v12 on v8

--- a/solution.py
+++ b/solution.py
@@ -72,6 +72,14 @@
         return (lax.rem(y + dy, SIDE) * SIDE + lax.rem(x + dx, SIDE), c)
 
     others = [(dy, dx) for dy in (2, 1, 3, 0) for dx in (2, 1, 3, 0) if (dy, dx) != (0, 0)]
+
+    barrier = pltpu.get_barrier_semaphore()
+    for to in [peer(dy, dx) for dy, dx in others] + [(t, c_near)]:
+        pl.semaphore_signal(barrier, inc=1, device_id=to, device_id_type=MESH)
+
+    @pl.when(has_far)
+    def _():
+        pl.semaphore_signal(barrier, inc=1, device_id=(t, c_far), device_id_type=MESH)
 
     skew = lax.rem(x - y + SIDE, SIDE)
     basis_copies = [
@@ -91,14 +99,6 @@
         rec_copies[q].start()
     pair_copy.start()
     live_copy.start()
-
-    barrier = pltpu.get_barrier_semaphore()
-    for to in [(t, c_near)] + [peer(dy, dx) for dy, dx in others]:
-        pl.semaphore_signal(barrier, inc=1, device_id=to, device_id_type=MESH)
-
-    @pl.when(has_far)
-    def _():
-        pl.semaphore_signal(barrier, inc=1, device_id=(t, c_far), device_id_type=MESH)
 
     @pl.when(jnp.logical_not(has_far))
     def _():
@@ -275,8 +275,8 @@
     before_a(3)
     forward_b(2)
     after_a(3)
+    forward_b(3)
     before_b(0)
-    forward_b(3)
     after_b(0)
     before_b(1)
     after_b(1)

time: 27 us -> 26.9 us (level)
  no operation moved by 1% of the time
where the time goes in v12:
time: 26.9 us; the launch traced here: 26.5 us
  Pallas kernels  25.2 us (94%)
  local copies, waits for them, and re-layouts  0.66 us (2%)
  between operations  0.66 us (2%)
    pallas_call x1, Pallas kernels, body(): pl.pallas_call(kernel, out_shape=vmem((2, 2 * BINS, PAIRS), f32), in_spec...  25.2 us
    unnamed x1, local copies, waits for them, and re-layouts  0.66 us

profile of v12, /device:TPU:1, one launch (start us, length us, event | category | flops | bytes accessed | tf_op | source)
XLA Modules:
  0.0 26.5 jit_solution(14420674732112564347)
XLA Ops:
  0.7 25.2 %shard_map.55 = f32[2,16,1024]{2,1,0:T(8,128)S(1)} custom-call(bf16[7,7,16,1024]{3,2,1,0:T(8,128)(2,1)} %constant.4.clone.basis_a_hbm, bf16[7,7,16,1024]{3,2,1,0:T(8,128)(2,1)} %constant.5.clone.basis_b_hbm, bf16[8,1024,128]{2,1,0:T(8,128)(2,1)} %rec_hbm.1, s32[2,1024]{1,0:T(2,128)} %pair_hbm.1, s32[1]{0:T(128)S(6)} %copy.8.live_hbm), custom_call_target="tpu_custom_call" | custom-call | flops 7000000000 | bytes 4194304 | tf_op jit(solution)/shard_map/pallas_call | solution.py:306
  25.8 0.7 %copy.7 = f32[2,16,1024]{2,1,0:T(8,128)} copy(f32[2,16,1024]{2,1,0:T(8,128)S(1)} %shard_map.55) | data formatting | bytes 262144

commit v13 on v3

--- a/solution.py
+++ b/solution.py
@@ -72,6 +72,14 @@
         return (lax.rem(y + dy, SIDE) * SIDE + lax.rem(x + dx, SIDE), c)
 
     others = [(dy, dx) for dy in (2, 1, 3, 0) for dx in (2, 1, 3, 0) if (dy, dx) != (0, 0)]
+
+    barrier = pltpu.get_barrier_semaphore()
+    for to in [peer(dy, dx) for dy, dx in others] + [(t, c_near)]:
+        pl.semaphore_signal(barrier, inc=1, device_id=to, device_id_type=MESH)
+
+    @pl.when(has_far)
+    def _():
+        pl.semaphore_signal(barrier, inc=1, device_id=(t, c_far), device_id_type=MESH)
 
     skew = lax.rem(x - y + SIDE, SIDE)
     basis_copies = [
@@ -91,14 +99,6 @@
         rec_copies[q].start()
     pair_copy.start()
     live_copy.start()
-
-    barrier = pltpu.get_barrier_semaphore()
-    for to in [(t, c_near)] + [peer(dy, dx) for dy, dx in others]:
-        pl.semaphore_signal(barrier, inc=1, device_id=to, device_id_type=MESH)
-
-    @pl.when(has_far)
-    def _():
-        pl.semaphore_signal(barrier, inc=1, device_id=(t, c_far), device_id_type=MESH)
 
     @pl.when(jnp.logical_not(has_far))
     def _():

time: 26.2 us -> 26.2 us (level)
  no operation moved by 1% of the time
where the time goes in v13:
time: 26.2 us; the launch traced here: 26.1 us
  Pallas kernels  24.7 us (94%)
  local copies, waits for them, and re-layouts  0.66 us (3%)
  between operations  0.66 us (3%)
    pallas_call x1, Pallas kernels, body(): pl.pallas_call(kernel, out_shape=vmem((2, 2 * BINS, PAIRS), f32), in_spec...  24.7 us
    unnamed x1, local copies, waits for them, and re-layouts  0.66 us

profile of v13, /device:TPU:1, one launch (start us, length us, event | category | flops | bytes accessed | tf_op | source)
XLA Modules:
  0.0 26.1 jit_solution(1442145939165413816)
XLA Ops:
  0.7 24.7 %shard_map.55 = f32[2,16,1024]{2,1,0:T(8,128)S(1)} custom-call(bf16[7,7,16,1024]{3,2,1,0:T(8,128)(2,1)} %constant.4.clone.basis_a_hbm, bf16[7,7,16,1024]{3,2,1,0:T(8,128)(2,1)} %constant.5.clone.basis_b_hbm, bf16[8,1024,128]{2,1,0:T(8,128)(2,1)} %rec_hbm.1, s32[2,1024]{1,0:T(2,128)} %pair_hbm.1, s32[1]{0:T(128)S(6)} %copy.8.live_hbm), custom_call_target="tpu_custom_call" | custom-call | flops 7000000000 | bytes 4194304 | tf_op jit(solution)/shard_map/pallas_call | solution.py:276
  25.4 0.7 %copy.7 = f32[2,16,1024]{2,1,0:T(8,128)} copy(f32[2,16,1024]{2,1,0:T(8,128)S(1)} %shard_map.55) | data formatting | bytes 262144
